TPU v7x, 128 devices: a whole 4x4x4 slice. The times are simulated.
128 devices in a mesh: lat: 16 (over z_lo, x, core), lon: 8 (over z_hi, y).
Axes of the slice: x: 4, y: 4, z: 4 (z_hi: 2, z_lo: 2; z = z_hi * 2 + z_lo), core: 2. Of those that a mesh axis runs over, the one named last changes fastest.
Arguments:
- tokens: bfloat16 [8, 96, 192, 192], P(None, 'lat', 'lon'), may hold values from -6 to 6
- lat_valid: int32 [96], P('lat'), may hold values from 0 to 1, as said below
- gain_attn: bfloat16 [192], replicated, may hold values from 0.099609375 to 1.8984375
- w_qkv: bfloat16 [192, 576], replicated, may hold values from -0.4375 to 0.4375
- w_proj: bfloat16 [192, 192], replicated, may hold values from -0.4375 to 0.4375
- gain_mlp: bfloat16 [192], replicated, may hold values from 0.099609375 to 1.8984375
- w_up: bfloat16 [192, 768], replicated, may hold values from -0.4375 to 0.4375
- w_down: bfloat16 [768, 192], replicated, may hold values from -0.21875 to 0.21875
- bias_table: float32 [64, 6, 3312], P('lat'), may hold values from -6 to 6
- index_table: int32 [144, 144], replicated, may hold values from 0 to 3311, as said below
- cotangent: bfloat16 [8, 96, 192, 192], P(None, 'lat', 'lon'), may hold values from -6 to 6
Outputs:
- updated: bfloat16 [8, 96, 192, 192], P(None, 'lat', 'lon')
- d_tokens: bfloat16 [8, 96, 192, 192], P(None, 'lat', 'lon')
- d_gain_attn: float32 [192], replicated
- d_qkv: float32 [192, 576], replicated
- d_proj: float32 [192, 192], replicated
- d_gain_mlp: float32 [192], replicated
- d_up: float32 [192, 768], replicated
- d_down: float32 [768, 192], replicated
- d_bias_table: float32 [64, 6, 3312], P('lat')
Inputs may be any that keep to these rules, and one draw needn't show every extreme that they name: `lat_valid`: 1 on every row but the last 1 to 5 rows, which are 0. `index_table`: every row of the bias table is named by some entry.
All inputs are finite; a program needn't handle non-finite values.
Results may differ from a plain program's by a relative error of at most 0.025.
Values may be sent and summed in bfloat16 or wider, within the bound.
A program may use at most 192 MiB of HBM per device.

v0:
```python
import jax
import jax.numpy as jnp
from jax import lax
from jax.sharding import PartitionSpec as P

WIN_Z = 2
WIN_LAT = 6
WIN_LON = 12


norm_eps = 1e-05


def shifted(value, axis, steps):
    count = lax.axis_size(axis)
    pairs = [(source, (source + steps) % count) for source in range(count)]
    return lax.ppermute(value, axis, pairs)


def product(form, left, right):
    return jnp.einsum(form, left, right, preferred_element_type=jnp.float32)


def layer_norm(inputs, norm_gain):
    inputs = inputs.astype(jnp.float32)
    center = inputs - jnp.mean(inputs, axis=-1, keepdims=True)
    rscale = lax.rsqrt(jnp.mean(center * center, axis=-1, keepdims=True) + norm_eps)
    return center * rscale * norm_gain.astype(jnp.float32)


def norm_back(inputs, norm_gain, incoming):
    inputs = inputs.astype(jnp.float32)
    center = inputs - jnp.mean(inputs, axis=-1, keepdims=True)
    rscale = lax.rsqrt(jnp.mean(center * center, axis=-1, keepdims=True) + norm_eps)
    normed = center * rscale
    scaled = incoming * norm_gain.astype(jnp.float32)
    d_inputs = rscale * (
        scaled
        - jnp.mean(scaled, axis=-1, keepdims=True)
        - normed * jnp.mean(scaled * normed, axis=-1, keepdims=True)
    )
    d_gain = jnp.sum((incoming * normed).reshape(-1, inputs.shape[-1]), axis=0)
    return (d_inputs, d_gain)


def to_windows(grid_field):
    levels, row_count, col_count, channels = grid_field.shape
    blocks = grid_field.reshape(
        levels // WIN_Z,
        WIN_Z,
        row_count // WIN_LAT,
        WIN_LAT,
        col_count // WIN_LON,
        WIN_LON,
        channels,
    )
    blocks = blocks.transpose(0, 2, 4, 1, 3, 5, 6)
    return blocks.reshape(
        levels // WIN_Z,
        row_count // WIN_LAT,
        col_count // WIN_LON,
        WIN_Z * WIN_LAT * WIN_LON,
        channels,
    )


def from_windows(blocks, levels, row_count, col_count):
    channels = blocks.shape[-1]
    blocks = blocks.reshape(
        levels // WIN_Z,
        row_count // WIN_LAT,
        col_count // WIN_LON,
        WIN_Z,
        WIN_LAT,
        WIN_LON,
        channels,
    )
    return blocks.transpose(0, 3, 1, 4, 2, 5, 6).reshape(levels, row_count, col_count, channels)


def window_regions(zone_count, last_band):
    positions = jnp.arange(WIN_Z * WIN_LAT * WIN_LON, dtype=jnp.int32)
    in_depth = positions // (WIN_LAT * WIN_LON)
    in_row = positions // WIN_LON % WIN_LAT
    zone_index = jnp.arange(zone_count, dtype=jnp.int32)[:, None]
    level_part = jnp.where(
        zone_index == zone_count - 1,
        1 + (in_depth[None, :] >= WIN_Z - WIN_Z // 2).astype(jnp.int32),
        0,
    )
    row_part = jnp.where(last_band, 1 + (in_row >= WIN_LAT - WIN_LAT // 2).astype(jnp.int32), 0)
    region = 3 * level_part + row_part[None, :]
    return (region[:, :, None] == region[:, None, :]).astype(jnp.float32)


def into_shifted(grid_field):
    row_half = WIN_LAT // 2
    col_half = WIN_LON // 2
    lower_rows = shifted(grid_field[:, :row_half], "lat", -1)
    grid_field = jnp.concatenate([grid_field[:, row_half:], lower_rows], axis=1)
    next_cols = shifted(grid_field[:, :, :col_half], "lon", -1)
    grid_field = jnp.concatenate([grid_field[:, :, col_half:], next_cols], axis=2)
    return jnp.roll(grid_field, -(WIN_Z // 2), axis=0)


def from_shifted(grid_field):
    row_half = WIN_LAT // 2
    col_half = WIN_LON // 2
    grid_field = jnp.roll(grid_field, WIN_Z // 2, axis=0)
    row_count = grid_field.shape[1]
    col_count = grid_field.shape[2]
    upper_rows = shifted(grid_field[:, row_count - row_half :], "lat", 1)
    grid_field = jnp.concatenate([upper_rows, grid_field[:, : row_count - row_half]], axis=1)
    prev_cols = shifted(grid_field[:, :, col_count - col_half :], "lon", 1)
    return jnp.concatenate([prev_cols, grid_field[:, :, : col_count - col_half]], axis=2)


def attend(windows, w_qkv, w_proj, pos_bias, allowed):
    window_count, places, channels = windows.shape
    head_count = pos_bias.shape[0]
    head_width = channels // head_count
    triple = product("bpc,cd->bpd", windows, w_qkv).astype(jnp.bfloat16)
    parted = triple.reshape(window_count, places, 3, head_count, head_width)
    queries, key_part, values = (parted[:, :, 0], parted[:, :, 1], parted[:, :, 2])
    scores = product("bqhd,bkhd->bhqk", queries, key_part) * head_width ** (-0.5) + pos_bias[None]
    weights = jnp.exp(scores) * allowed[None, None]
    chances = (weights / jnp.sum(weights, axis=-1, keepdims=True)).astype(jnp.bfloat16)
    merged = (
        product("bhqk,bkhd->bqhd", chances, values)
        .astype(jnp.bfloat16)
        .reshape(window_count, places, channels)
    )
    attended = product("bpc,cd->bpd", merged, w_proj).astype(jnp.bfloat16)
    return (attended, triple, chances, merged)


def attend_back(incoming, windows, triple, chances, merged, w_qkv, w_proj):
    window_count, places, channels = windows.shape
    head_count = chances.shape[1]
    head_width = channels // head_count
    d_proj = product("bpc,bpd->cd", merged, incoming)
    d_merged = (
        product("bpd,cd->bpc", incoming, w_proj)
        .astype(jnp.bfloat16)
        .reshape(window_count, places, head_count, head_width)
    )
    parted = triple.reshape(window_count, places, 3, head_count, head_width)
    queries, key_part, values = (parted[:, :, 0], parted[:, :, 1], parted[:, :, 2])
    d_chances = product("bqhd,bkhd->bhqk", d_merged, values)
    d_values = product("bhqk,bqhd->bkhd", chances, d_merged)
    chance_f = chances.astype(jnp.float32)
    d_scores = chance_f * (d_chances - jnp.sum(chance_f * d_chances, axis=-1, keepdims=True))
    scaled = (d_scores * head_width ** (-0.5)).astype(jnp.bfloat16)
    d_queries = product("bhqk,bkhd->bqhd", scaled, key_part)
    d_keys = product("bhqk,bqhd->bkhd", scaled, queries)
    d_triple = (
        jnp.stack([d_queries, d_keys, d_values], axis=2)
        .astype(jnp.bfloat16)
        .reshape(window_count, places, 3 * channels)
    )
    d_qkv = product("bpc,bpd->cd", windows, d_triple)
    d_windows = product("bpd,cd->bpc", d_triple, w_qkv).astype(jnp.bfloat16)
    return (d_windows, d_qkv, d_proj, jnp.sum(d_scores, axis=0))


def table_grad(score_sums, index_flat, entries):
    zone_count, head_count = (score_sums.shape[0], score_sums.shape[1])
    flat_scores = score_sums.reshape(zone_count * head_count, -1).T
    summed = jax.ops.segment_sum(flat_scores, index_flat, num_segments=entries)
    return summed.T.reshape(zone_count, head_count, entries)


def mlp_block(residual, gain_mlp, w_up, w_down):
    second_norm = layer_norm(residual, gain_mlp).astype(jnp.bfloat16)
    hidden_pre = jnp.dot(second_norm, w_up, preferred_element_type=jnp.float32)
    hidden = jax.nn.gelu(hidden_pre).astype(jnp.bfloat16)
    lifted = jnp.dot(hidden, w_down, preferred_element_type=jnp.float32)
    return (second_norm, hidden_pre, hidden, lifted)


def mlp_back(second_norm, hidden_pre, hidden, residual, gain_mlp, w_up, w_down, upstream):
    d_down = jnp.dot(hidden.T, upstream, preferred_element_type=jnp.float32)
    d_hidden = jnp.dot(upstream, w_down.T, preferred_element_type=jnp.float32)
    d_pre = jax.vjp(jax.nn.gelu, hidden_pre)[1](d_hidden)[0].astype(jnp.bfloat16)
    d_up = jnp.dot(second_norm.T, d_pre, preferred_element_type=jnp.float32)
    d_norm = jnp.dot(d_pre, w_up.T, preferred_element_type=jnp.float32)
    d_resid, d_gain = norm_back(residual, gain_mlp, d_norm)
    return (d_resid + upstream.astype(jnp.float32), d_up, d_down, d_gain)


def per_device(
    tokens,
    lat_valid,
    gain_attn,
    w_qkv,
    w_proj,
    gain_mlp,
    w_up,
    w_down,
    bias_table,
    index_table,
    cotangent,
):
    levels, row_count, col_count, channels = tokens.shape
    zone_count = levels // WIN_Z
    places = WIN_Z * WIN_LAT * WIN_LON
    entries = bias_table.shape[2]
    lat_count = lax.axis_size("lat")
    last_band = lax.axis_index("lat") == lat_count - 1
    grad_scale = float(levels * row_count * col_count * lat_count * lax.axis_size("lon")) ** (-0.5)
    keep_rows = (lat_valid > 0)[None, :, None, None]
    inputs = jnp.where(keep_rows, tokens, jnp.zeros_like(tokens))
    upstream = jnp.where(keep_rows, cotangent, jnp.zeros_like(cotangent))
    index_flat = index_table.reshape(-1)
    pos_bias = jnp.take(bias_table, index_flat, axis=2).reshape(zone_count, -1, places, places)
    allowed = window_regions(zone_count, last_band)

    def forward_pass(block_inputs):
        first_norm = layer_norm(block_inputs, gain_attn).astype(jnp.bfloat16)
        windows = to_windows(into_shifted(first_norm))[:, 0]

        def zone_forward(zone_parts):
            return attend(zone_parts[0], w_qkv, w_proj, zone_parts[1], zone_parts[2])

        attended, triple, chances, merged = lax.map(zone_forward, (windows, pos_bias, allowed))
        attn_out = from_shifted(from_windows(attended[:, None], levels, row_count, col_count))
        residual = (block_inputs.astype(jnp.float32) + attn_out.astype(jnp.float32)).astype(
            jnp.bfloat16
        )
        second_norm, hidden_pre, hidden, lifted = mlp_block(
            residual.reshape(-1, channels), gain_mlp, w_up, w_down
        )
        result = jnp.where(
            keep_rows, residual.astype(jnp.float32) + lifted.reshape(residual.shape), 0.0
        ).astype(jnp.bfloat16)
        return (
            result,
            (windows, triple, chances, merged, residual, second_norm, hidden_pre, hidden),
        )

    updated, kept_state = forward_pass(inputs)
    inputs_again, upstream = lax.optimization_barrier((inputs, upstream))
    kept_state = forward_pass(inputs_again)[1]
    windows, triple, chances, merged, residual, second_norm, hidden_pre, hidden = kept_state
    d_resid, d_up, d_down, d_gain_mlp = mlp_back(
        second_norm,
        hidden_pre,
        hidden,
        residual.reshape(-1, channels),
        gain_mlp,
        w_up,
        w_down,
        upstream.reshape(-1, channels),
    )
    d_up = d_up * grad_scale
    d_down = d_down * grad_scale
    d_gain_mlp = d_gain_mlp * grad_scale
    d_residual = d_resid.reshape(tokens.shape)
    d_incoming = to_windows(into_shifted(d_residual.astype(jnp.bfloat16)))[:, 0]

    def zone_back(zone_parts):
        return attend_back(
            zone_parts[0], zone_parts[1], zone_parts[2], zone_parts[3], zone_parts[4], w_qkv, w_proj
        )

    d_wins, d_qkv_z, d_proj_z, d_score_z = lax.map(
        zone_back, (d_incoming, windows, triple, chances, merged)
    )
    d_table = lax.psum(
        (table_grad(d_score_z, index_flat, entries) * grad_scale).astype(jnp.bfloat16), "lon"
    ).astype(jnp.float32)
    d_first = from_shifted(from_windows(d_wins[:, None], levels, row_count, col_count))
    d_inputs, d_gain_attn = norm_back(inputs, gain_attn, d_first.astype(jnp.float32))
    d_tokens = jnp.where(keep_rows, d_residual + d_inputs, 0.0).astype(jnp.bfloat16)
    d_qkv = jnp.sum(d_qkv_z, axis=0) * grad_scale
    d_proj = jnp.sum(d_proj_z, axis=0) * grad_scale
    d_gain_attn = d_gain_attn * grad_scale
    d_gain_attn, d_qkv, d_proj, d_gain_mlp, d_up, d_down = lax.psum(
        (d_gain_attn, d_qkv, d_proj, d_gain_mlp, d_up, d_down), ("lat", "lon")
    )
    return (updated, d_tokens, d_gain_attn, d_qkv, d_proj, d_gain_mlp, d_up, d_down, d_table)


def solution(mesh):
    in_specs = (
        P(None, "lat", "lon", None),
        P("lat"),
        P(),
        P(),
        P(),
        P(),
        P(),
        P(),
        P("lat", None, None),
        P(),
        P(None, "lat", "lon", None),
    )
    out_specs = (
        P(None, "lat", "lon", None),
        P(None, "lat", "lon", None),
        P(),
        P(),
        P(),
        P(),
        P(),
        P(),
        P("lat", None, None),
    )
    return jax.shard_map(
        per_device, mesh=mesh, in_specs=in_specs, out_specs=out_specs, check_vma=False
    )
```

profile of v0, /device:TPU:0, one launch (start us, length us, event | category | flops | bytes accessed | tf_op | source)
XLA Modules:
  0.0 719.5 jit_solution(3983639342740741264)
XLA Ops:
  13.5 3.7 collective-permute-start.4
  17.5 4.8 copy.206
  22.6 60.8 %gather_fusion = f32[20736,4,6]{2,1,0:T(4,128)} fusion(f32[4,6,3312]{1,0,2:T(4,128)} %copy.206, s32[21504]{0:T(1024)S(1)} %pad_clamp_fusion), kind=kCustom, calls=%fused_computation | custom fusion | bytes 4064256 | tf_op jit(solution)/shard_map/jit(_take)/gather | solution.py:215
  83.3 42.5 %copy.257 = f32[4,6,144,144]{3,2,0,1:T(8,128)} copy(f32[4,6,144,144]{1,0,3,2:T(4,128)} %bitcast.340) | data formatting | bytes 3981312 | tf_op jit(solution)/shard_map/jit(_take)/gather | solution.py:215
  125.8 4.2 broadcast_select_fusion
  130.0 5.6 copy.209
  136.7 6.4 collective-permute-start.5
  149.2 44.5 %while.43 = (s32[]{:T(128)}, bf16[4,2,144,192]{3,1,2,0:T(2,128)(2,1)}, bf16[4,2,144,576]{3,2,1,0:T(8,128)(2,1)}, bf16[4,2,6,144,144]{3,4,2,1,0:T(8,128)(2,1)}, b...) while((s32[]{:T(128)}, ...), condition=%wide.region_11.12_spmd, body=%wide.region_9.11_spmd.sunk | while | flops 118307664 | bytes 7928437 | solution.py:225
  154.5 2.9 bitcast_dynamic-update-slice_fusion.5
  176.7 2.9 bitcast_dynamic-update-slice_fusion.5
  196.8 7.8 %collective-permute-done.6 = bf16[8,3,24,192]{3,0,2,1:T(8,128)(2,1)S(1)} collective-permute-done((bf16[8,3,24,192]{3,0,2,1:T(8,128)(2,1)S(1)}, bf16[8,3,24,192]{3,0,2,1:T(8,128)(2,1)S(1)}, u32[]{:S(2)}, u32[]{:S(2)}) %collective-permute-start.6) | collective-permute-done | bytes 221216 | tf_op jit(solution)/shard_map/ppermute | solution.py:17
  208.4 7.0 collective-permute-done.7
  232.9 3.5 collective-permute-done.9
  238.9 90.6 %while.44 = (s32[]{:T(128)}, bf16[4,2,144,192]{3,1,2,0:T(2,128)(2,1)}, f32[4,192,576]{2,1,0:T(8,128)}, f32[4,192,192]{2,1,0:T(8,128)}, f32[4,6,144,144]{3,2,1,0:...) while((s32[]{:T(128)}, ...), condition=%wide.region_19.20_spmd, body=%wide.region_16.19_spmd.sunk | while | flops 238870512 | bytes 34235124 | solution.py:266
  333.5 5.0 reshape.376
  338.6 6.9 copy.242
  345.5 112.8 %scatter_custom_fusion = f32[3312,24]{1,0:T(8,128)S(1)} fusion(s32[20736]{0:T(1024)} %reshape.389, f32[20736,24]{1,0:T(8,128)} %copy.242, f32[]{:T(128)} %constant.143.clone.1), kind=kCustom, calls=%fused_computation.155 | custom fusion | flops 497664 | bytes 318464 | tf_op jit(solution)/shard_map/scatter-add | solution.py:169
  472.1 4.6 collective-permute-start
  477.5 3.4 collective-permute-done
  480.9 4.2 collective-permute-start.1
  491.2 29.3 %while.42 = (s32[]{:T(128)}, bf16[4,2,144,192]{3,1,2,0:T(2,128)(2,1)}, bf16[4,2,144,192]{3,1,2,0:T(2,128)(2,1)}, bf16[192,576]{1,0:T(8,128)(2,1)S(1)}, f32[4,6,1...) while((s32[]{:T(128)}, bf16[4,2,144,192]{3,1,2,0:T(2,128)(2,1)}, ...), condition=%wide.region_4.5_spmd, body=%wide.region_2.4_spmd.sunk | while | flops 118307664 | bytes 9529953 | solution.py:225
  523.8 26.9 %all-reduce.5.cloned.1.call-done = bf16[4,6,3312]{2,1,0:T(8,128)(2,1)} async-done(((bf16[4,6,3312]{2,1,0:T(8,128)(2,1)}), bf16[4,6,3312]{2,1,0:T(8,128)(2,1)}) %all-reduce.5.cloned.1.call-update) | async-done | bytes 158992 | tf_op jit(solution)/shard_map/psum | solution.py:269
  554.8 64.4 %all-reduce = (f32[192]{0:T(256)}, f32[192]{0:T(256)}) all-reduce(f32[192]{0:T(256)S(1)} %broadcast_multiply_fusion.11, f32[192]{0:T(256)S(1)} %copy-done.28), channel_id=1, replica_groups=mesh['lat'=16,'lon'=8] {'lat','lon'}, use_global_device_ids=true, to_apply=%region_23.24 | all-reduce | flops 384 | bytes 3072 | tf_op jit(solution)/shard_map/psum | solution.py:278
  624.2 82.9 %all-reduce.7.cloned.1.call-done = (f32[192,576]{1,0:T(8,128)}, f32[192,192]{1,0:T(8,128)}, f32[192,768]{1,0:T(8,128)}, f32[768,192]{0,1:T(8,128)}) async-done(((f32[192,576]{1,0:T(8,128)}, f32[192,192]{1,0:T(8,128)}, f32[192,768]{1,0:T(8,128)}, f32[768,192]{0,1:T(8,128)}), (f32[192,576]{1,0:T(8,128)}, f32[192,192]{1,0:T(8,128)}, f32[192,768]{1,0:T(8,128)}, ...) | async-done | bytes 1769488 | tf_op jit(solution)/shard_map/psum | solution.py:278
  (379 shorter events, 240.6 us)
Async XLA Ops:
  7.2 211.0 %copy-start = (bf16[192,768]{1,0:T(8,128)(2,1)S(1)}, bf16[192,768]{1,0:T(8,128)(2,1)}, u32[]{:S(2)}) copy-start(bf16[192,768]{1,0:T(8,128)(2,1)} %param.23) | copy-start | bytes 884740
  7.2 543.6 %all-reduce.5.cloned.1.call-start = ((), (), s32[]{:S(2)}) async-start(), calls=%async_computation | async-start | bytes 425984 | tf_op jit(solution)/shard_map/psum | solution.py:269
  10.0 205.4 %copy-start.2 = (bf16[8,6,24,192]{3,0,2,1:T(8,128)(2,1)}, bf16[8,6,24,192]{3,0,2,1:T(8,128)(2,1)S(1)}, u32[]{:S(2)}) copy-start(bf16[8,6,24,192]{3,0,2,1:T(8,128)(2,1)S(1)} %get-tuple-element.169) | copy-start | bytes 1327108
  13.5 123.2 %collective-permute-start.4 = (bf16[8,3,24,192]{3,0,2,1:T(8,128)(2,1)S(1)}, bf16[8,3,24,192]{3,0,2,1:T(8,128)(2,1)S(1)}, u32[]{:S(2)}, u32[]{:S(2)}) collective-permute-start(bf16[8,3,24,192]{3,0,2,1:T(8,128)(2,1)S(1)} %get-tuple-element.401), channel_id=1, source_target_pairs={{0,120},{8,0},{16,8},{24,16},{32,24},{40,32},{48,40},{56,48},{64,5... | collective-permute-start | bytes 663560 | tf_op jit(solution)/shard_map/ppermute | solution.py:17
  136.7 9.1 %collective-permute-start.5 = (bf16[8,6,6,192]{3,0,2,1:T(8,128)(2,1)S(1)}, bf16[8,6,6,192]{3,0,2,1:T(8,128)(2,1)S(1)}, u32[]{:S(2)}, u32[]{:S(2)}) collective-permute-start(bf16[8,6,6,192]{3,0,2,1:T(8,128)(2,1)S(1)} %pad_maximum_fusion.12), channel_id=1, source_target_pairs={{0,7},{1,0},{2,1},{3,2},{4,3},{5,4},{6,5},{7,6},{8,15},{9,8},{10,9... | collective-permute-start | bytes 331784 | tf_op jit(solution)/shard_map/ppermute | solution.py:17
  196.1 11.2 %copy-start.32 = (bf16[192]{0:T(256)(128)(2,1)S(1)}, bf16[192]{0:T(256)(128)(2,1)}, u32[]{:S(2)}) copy-start(bf16[192]{0:T(256)(128)(2,1)} %param.22) | copy-start | bytes 1156
  196.1 11.2 %copy-start.13 = (bf16[8,6,24,192]{3,0,2,1:T(8,128)(2,1)S(1)}, bf16[8,6,24,192]{3,0,2,1:T(8,128)(2,1)}, u32[]{:S(2)}) copy-start(bf16[8,6,24,192]{3,0,2,1:T(8,128)(2,1)} %copy_select_fusion) | copy-start | bytes 1327108
  196.3 8.3 %collective-permute-start.6 = (bf16[8,3,24,192]{3,0,2,1:T(8,128)(2,1)S(1)}, bf16[8,3,24,192]{3,0,2,1:T(8,128)(2,1)S(1)}, u32[]{:S(2)}, u32[]{:S(2)}) collective-permute-start(bf16[8,3,24,192]{3,0,2,1:T(8,128)(2,1)S(1)} %fusion.103), channel_id=1, source_target_pairs={{0,8},{8,16},{16,24},{24,32},{32,40},{40,48},{48,56},{56,64},{64,7... | collective-permute-start | bytes 663560 | tf_op jit(solution)/shard_map/ppermute | solution.py:17
  196.4 10.9 %copy-start.20 = (f32[8,6,24]{0,2,1:T(8,128)}, f32[8,6,24]{0,2,1:T(8,128)S(1)}, u32[]{:S(2)}) copy-start(f32[8,6,24]{0,2,1:T(8,128)S(1)} %broadcast_multiply_fusion.7) | copy-start | bytes 13828
  205.3 10.0 %collective-permute-start.7 = (bf16[8,6,6,192]{3,0,2,1:T(8,128)(2,1)}, bf16[8,6,6,192]{3,0,2,1:T(8,128)(2,1)}, u32[]{:S(2)}, u32[]{:S(2)}) collective-permute-start(bf16[8,6,6,192]{3,0,2,1:T(8,128)(2,1)} %pad_maximum_fusion.11), channel_id=1, source_target_pairs={{0,1},{1,2},{2,3},{3,4},{4,5},{5,6},{6,7},{7,0},{8,9},{9,10},{10,1... | collective-permute-start | bytes 331784 | tf_op jit(solution)/shard_map/ppermute | solution.py:17
  226.1 4.3 collective-permute-start.8
  230.4 5.9 collective-permute-start.9
  331.9 126.5 %copy-start.11 = (bf16[1,6,24,192]{3,0,2,1:T(2,128)(2,1)}, bf16[1,6,24,192]{3,0,2,1:T(2,128)(2,1)S(1)}, u32[]{:S(2)}) copy-start(bf16[1,6,24,192]{3,0,2,1:T(2,128)(2,1)S(1)} %slice.212) | copy-start | bytes 165892
  332.8 125.6 %collective-permute-start.10 = (bf16[8,3,24,192]{3,0,2,1:T(8,128)(2,1)}, bf16[8,3,24,192]{3,0,2,1:T(8,128)(2,1)S(1)}, u32[]{:S(2)}, u32[]{:S(2)}) collective-permute-start(bf16[8,3,24,192]{3,0,2,1:T(8,128)(2,1)} %fusion.102), channel_id=1, source_target_pairs={{0,8},{8,16},{16,24},{24,32},{32,40},{40,48},{48,56},{56,64},{64,7... | collective-permute-start | bytes 663560 | tf_op jit(solution)/shard_map/ppermute | solution.py:17
  459.1 9.1 %collective-permute-start.11 = (bf16[8,6,6,192]{3,0,2,1:T(8,128)(2,1)}, bf16[8,6,6,192]{3,0,2,1:T(8,128)(2,1)}, u32[]{:S(2)}, u32[]{:S(2)}) collective-permute-start(bf16[8,6,6,192]{3,0,2,1:T(8,128)(2,1)} %pad_maximum_fusion.10), channel_id=1, source_target_pairs={{0,1},{1,2},{2,3},{3,4},{4,5},{5,6},{6,7},{7,0},{8,9},{9,10},{10,1... | collective-permute-start | bytes 331784 | tf_op jit(solution)/shard_map/ppermute | solution.py:17
  461.9 6.3 copy-start.3
  461.9 6.2 copy-start.12
  466.6 240.4 %all-reduce.7.cloned.1.call-start = ((), (), s32[]{:S(2)}) async-start(), calls=%async_computation.1 | async-start | bytes 3735552 | tf_op jit(solution)/shard_map/psum | solution.py:278
  472.1 8.8 %collective-permute-start = (bf16[8,3,24,192]{3,0,2,1:T(8,128)(2,1)S(1)}, bf16[8,3,24,192]{3,0,2,1:T(8,128)(2,1)S(1)}, u32[]{:S(2)}, u32[]{:S(2)}) collective-permute-start(bf16[8,3,24,192]{3,0,2,1:T(8,128)(2,1)S(1)} %get-tuple-element.403), channel_id=1, source_target_pairs={{0,120},{8,0},{16,8},{24,16},{32,24},{40,32},{48,40},{56,48},{64,5... | collective-permute-start | bytes 663560 | tf_op jit(solution)/shard_map/ppermute | solution.py:17
  480.9 6.9 collective-permute-start.1
  523.0 29.5 %collective-permute-start.2 = (bf16[8,3,24,192]{3,0,2,1:T(8,128)(2,1)S(1)}, bf16[8,3,24,192]{3,0,2,1:T(8,128)(2,1)S(1)}, u32[]{:S(2)}, u32[]{:S(2)}) collective-permute-start(bf16[8,3,24,192]{3,0,2,1:T(8,128)(2,1)S(1)} %fusion.104), channel_id=1, source_target_pairs={{0,8},{8,16},{16,24},{24,32},{32,40},{40,48},{48,56},{56,64},{64,7... | collective-permute-start | bytes 663560 | tf_op jit(solution)/shard_map/ppermute | solution.py:17
  523.8 30.1 %copy-start.14 = (bf16[8,6,24,192]{3,0,2,1:T(8,128)(2,1)S(1)}, bf16[8,6,24,192]{3,0,2,1:T(8,128)(2,1)}, u32[]{:S(2)}) copy-start(bf16[8,6,24,192]{3,0,2,1:T(8,128)(2,1)} %get-tuple-element.396) | copy-start | bytes 1327108
  523.8 31.0 %copy-start.28 = (f32[192]{0:T(256)S(1)}, f32[192]{0:T(256)}, u32[]{:S(2)}) copy-start(f32[192]{0:T(256)} %broadcast_multiply_fusion.10) | copy-start | bytes 2308
  552.5 66.7 %collective-permute-start.3 = (bf16[8,6,6,192]{3,0,2,1:T(8,128)(2,1)S(1)}, bf16[8,6,6,192]{3,0,2,1:T(8,128)(2,1)S(1)}, u32[]{:S(2)}, u32[]{:S(2)}) collective-permute-start(bf16[8,6,6,192]{3,0,2,1:T(8,128)(2,1)S(1)} %pad_maximum_fusion.13), channel_id=1, source_target_pairs={{0,1},{1,2},{2,3},{3,4},{4,5},{5,6},{6,7},{7,0},{8,9},{9,10},{10,1... | collective-permute-start | bytes 331784 | tf_op jit(solution)/shard_map/ppermute | solution.py:17
  (35 other events, 96.0 us)
Sparse Core Ops, SparseCore 0:
  466.7 83.9 all-reduce.4
  557.7 149.3 all-reduce.6
where the time goes:
time: 731 us; the launch traced here: 720 us
  local copies, waits for them, and re-layouts  223 us (31%)
  other arithmetic  157 us (21%)
  waiting for transfers between devices  139 us (19%)
  matrix products  95.9 us (13%)
  blocking collectives  64.4 us (9%)
  starting transfers between devices  23.5 us (3%)
  between operations  15.3 us (2%)
    scatter-add x1, other arithmetic, table_grad(): summed = jax.ops.segment_sum(flat_scores, index_flat, num_segments=entries)  113 us
    gather x2, local copies, waits for them, and re-layouts, per_device(): jnp.take(bias_table, index_flat, axis=2)  103 us
    psum x1, waiting for transfers between devices, per_device(): lax.psum((d_gain_attn, d_qkv, d_proj, d_gain_mlp, d_up, d_down), ('lat',...  82.9 us
    dot_general x60, matrix products, product(): return jnp.einsum(form, left, right, preferred_element_type=jnp.float32)  74.8 us
    psum x1, blocking collectives, per_device(): lax.psum((d_gain_attn, d_qkv, d_proj, d_gain_mlp, d_up, d_down), ('lat',...  64.4 us
    ppermute x12, waiting for transfers between devices, shifted(): return lax.ppermute(value, axis, pairs)  29.5 us
    psum x1, waiting for transfers between devices, per_device(): lax.psum((table_grad(d_score_z, index_flat, entries) * grad_scale).astype...  26.9 us
    ppermute x12, starting transfers between devices, shifted(): return lax.ppermute(value, axis, pairs)  23.4 us
  transfers between devices with their start and end apart: 14, of which 10 were waited for; matrix products, arithmetic and copies ran while one was open for 42% of the time, Pallas kernels for 0%

commit v1 on v0

v1 whole, which is shorter than its diff:
```python
import functools
import jax
import jax.numpy as jnp
from jax import lax
from jax.sharding import PartitionSpec as P
from jax.experimental import pallas as pl
from jax.experimental.pallas import tpu as pltpu

WIN_Z = 2
WIN_LAT = 6
WIN_LON = 12
PLACES = 144
HEADS = 6
WIDTH = 32
CH = 192
HIDDEN = 768
WINDOWS = 8
TOKENS = 1152
ZONES = 4
ROWS = ZONES * HEADS
ENTRIES = 3312
HI = 13
GROUPS = 18
SPAN = 1152
LOG2E = 1.4426950408889634
SCALE = 32**-0.5
NORM_EPS = 1e-05
F32 = jnp.float32
BF16 = jnp.bfloat16


def dot(left, right, left_dim=1, right_dim=0):
    return lax.dot_general(
        left, right, (((left_dim,), (right_dim,)), ((), ())), preferred_element_type=F32
    )


def entry_lanes(idx_ref, group):
    start = pl.multiple_of(group * 8, 8)
    main = idx_ref[pl.ds(start, 8), 0:128]
    rest = idx_ref[pl.ds(start, 8), 128:256].astype(F32)
    rest = pltpu.roll(rest, 0, 1, stride=16, stride_axis=0)
    place = lax.broadcasted_iota(jnp.int32, (8, 128), 0)
    lane = lax.broadcasted_iota(jnp.int32, (8, 128), 1)
    rest = jnp.sum(jnp.where(lane // 16 == place, rest, 0.0), axis=0, keepdims=True)
    rows = [main[i : i + 1] for i in range(8)] + [rest.astype(jnp.int32)]
    return jnp.concatenate(rows, axis=1)


def low_onehot(entries):
    low = jnp.broadcast_to(entries & 255, (256, SPAN))
    at = lax.broadcasted_iota(jnp.int32, (256, SPAN), 0)
    return jnp.where(low == at, 1.0, 0.0).astype(BF16)


def transposed_index(idx_in, idx_ref):
    idx_ref[:, 128:256] = jnp.zeros((PLACES, 128), jnp.int32)
    flipped = jnp.transpose(idx_in[...].astype(F32)).astype(jnp.int32)
    idx_ref[:, 0:PLACES] = flipped


def region_of(place, last_zone, last_band):
    depth = place // (WIN_LAT * WIN_LON)
    row = place // WIN_LON % WIN_LAT
    level = jnp.where(depth >= WIN_Z - WIN_Z // 2, 2, 1) * last_zone
    band = jnp.where(row >= WIN_LAT - WIN_LAT // 2, 2, 1) * last_band
    return 3 * level + band


def gather_kernel(last_ref, table_ref, idx_in, bias_ref, idx_ref, t2_ref):
    transposed_index(idx_in, idx_ref)
    for hi in range(HI):
        wide = min(256, ENTRIES - hi * 256)
        for zone in range(ZONES):
            part = table_ref[zone, :, hi * 256 : hi * 256 + wide] * LOG2E
            if wide < 256:
                part = jnp.concatenate([part, jnp.zeros((HEADS, 256 - wide), F32)], axis=1)
            t2_ref[hi * ROWS + zone * HEADS : hi * ROWS + (zone + 1) * HEADS, :] = part
    last_band = last_ref[0]

    def step(group, carry):
        entries = entry_lanes(idx_ref, group)
        onehot = low_onehot(entries)
        found = dot(t2_ref[...].astype(BF16), onehot)
        high = jnp.broadcast_to(entries >> 8, (ROWS, SPAN))
        bias = jnp.where(high == 0, found[0:ROWS], 0.0)
        for hi in range(1, HI):
            bias = jnp.where(high == hi, found[hi * ROWS : (hi + 1) * ROWS], bias)
        lane = lax.broadcasted_iota(jnp.int32, (ROWS, 128), 1)
        zone3 = (lax.broadcasted_iota(jnp.int32, (ROWS, 128), 0) >= ROWS - HEADS).astype(jnp.int32)
        rest = bias[:, 1024:1152]
        for i in range(8):
            key = group * 8 + i
            key_region = region_of(jnp.full((ROWS, 128), key, jnp.int32), zone3, last_band)
            main_ok = region_of(lane, zone3, last_band) == key_region
            rest_ok = region_of((lane & 15) + 128, zone3, last_band) == key_region
            main_i = jnp.where(main_ok, bias[:, i * 128 : (i + 1) * 128], -1e30)
            rest_i = rest if i == 0 else pltpu.roll(rest, 128 - 16 * i, 1)
            rest_i = jnp.where(rest_ok, rest_i, -1e30)
            bias_ref[0, pl.ds(key, ROWS, stride=PLACES), :] = main_i
            bias_ref[1, pl.ds(key, ROWS, stride=PLACES), :] = rest_i
        return carry

    lax.fori_loop(0, GROUPS, step, 0)


def scatter_kernel(ds_ref, idx_in, out_ref, idx_ref, acc_ref):
    transposed_index(idx_in, idx_ref)
    acc_ref[...] = jnp.zeros_like(acc_ref)
    lane = lax.broadcasted_iota(jnp.int32, (ROWS, 128), 1)

    def step(group, carry):
        entries = entry_lanes(idx_ref, group)
        onehot = low_onehot(entries)
        mains, rest = [], jnp.zeros((ROWS, 128), F32)
        for i in range(8):
            key = group * 8 + i
            mains.append(ds_ref[0, pl.ds(key, ROWS, stride=PLACES), :])
            rest_i = ds_ref[1, pl.ds(key, ROWS, stride=PLACES), :]
            if i:
                rest_i = pltpu.roll(rest_i, 16 * i, 1)
            rest = jnp.where(lane // 16 == i, rest_i, rest)
        grads = jnp.concatenate(mains + [rest], axis=1)
        high = jnp.broadcast_to(entries >> 8, (ROWS, SPAN))
        parts = [jnp.where(high == hi, grads, 0.0) for hi in range(HI)]
        left = jnp.concatenate(parts, axis=0).astype(BF16)
        acc_ref[...] += dot(left, onehot, 1, 1)
        return carry

    lax.fori_loop(0, GROUPS, step, 0)
    out_ref[...] = acc_ref[...]


def normed(values):
    center = values - jnp.mean(values, axis=-1, keepdims=True)
    rscale = lax.rsqrt(jnp.mean(center * center, axis=-1, keepdims=True) + NORM_EPS)
    return center * rscale, rscale


def norm_back(unit, rscale, gain, incoming):
    scaled = incoming * gain
    d_inputs = rscale * (
        scaled
        - jnp.mean(scaled, axis=-1, keepdims=True)
        - unit * jnp.mean(scaled * unit, axis=-1, keepdims=True)
    )
    return d_inputs, jnp.sum(incoming * unit, axis=0, keepdims=True)


def main_kernel(
    grad_scale,
    xw_ref,
    cw_ref,
    bias_ref,
    g1_ref,
    wqkv_ref,
    wproj_ref,
    g2_ref,
    wup_ref,
    wdown_ref,
    upd_ref,
    dtok_ref,
    dgain_ref,
    dqkv_ref,
    dproj_ref,
    dup_ref,
    ddown_ref,
    ds_ref,
    wqkvt_s,
    soft_s,
    trip_s,
    mrg_s,
    inv_s,
    first_s,
    resid_s,
    dres_s,
    dtrip_s,
):
    wqkvt_s[...] = jnp.transpose(wqkv_ref[...].astype(F32)).astype(BF16)
    g1 = g1_ref[...].astype(F32)
    g2 = g2_ref[...].astype(F32)

    def forward(w, carry):
        rows = pl.ds(pl.multiple_of(w * PLACES, PLACES), PLACES)
        x = xw_ref[rows, :].astype(F32)
        first = (normed(x)[0] * g1).astype(BF16)
        first_s[rows, :] = first
        triple = dot(wqkvt_s[...], first, 1, 1)
        trip_s[w, 0:CH] = (triple[0:CH] * (SCALE * LOG2E)).astype(BF16)
        trip_s[w, CH : 3 * CH] = triple[CH : 3 * CH].astype(BF16)
        zone = w // 2
        for h in range(HEADS):
            query = trip_s[w, h * WIDTH : (h + 1) * WIDTH]
            keys = trip_s[w, CH + h * WIDTH : CH + (h + 1) * WIDTH]
            values = trip_s[w, 2 * CH + h * WIDTH : 2 * CH + (h + 1) * WIDTH]
            at = pl.ds(pl.multiple_of((zone * HEADS + h) * PLACES, PLACES), PLACES)
            bias = jnp.concatenate([bias_ref[0, at, :], bias_ref[1, at, 0:16]], axis=1)
            scores = dot(keys, query, 0, 0) + bias
            weights = jnp.exp2(scores - jnp.max(scores, axis=0, keepdims=True))
            inv = 1.0 / jnp.sum(weights, axis=0, keepdims=True)
            weights = weights.astype(BF16)
            soft_s[w * HEADS + h] = weights
            inv_s[w, h : h + 1] = inv
            mrg_s[w, h * WIDTH : (h + 1) * WIDTH] = (dot(values, weights) * inv).astype(BF16)
        attended = dot(mrg_s[w], wproj_ref[...], 0, 0).astype(BF16).astype(F32)
        resid_s[rows, :] = (x + attended).astype(BF16)
        return carry

    lax.fori_loop(0, WINDOWS, forward, 0)

    dgain_ref[...] = jnp.zeros_like(dgain_ref)
    dqkv_ref[...] = jnp.zeros_like(dqkv_ref)
    dproj_ref[...] = jnp.zeros_like(dproj_ref)
    dup_ref[...] = jnp.zeros_like(dup_ref)
    ddown_ref[...] = jnp.zeros_like(ddown_ref)

    chunk = 384

    def feed_forward(c, carry):
        rows = pl.ds(pl.multiple_of(c * chunk, chunk), chunk)
        resid = resid_s[rows, :].astype(F32)
        up = cw_ref[rows, :]
        unit, rscale = normed(resid)
        second = unit * g2
        second_b = second.astype(BF16)
        pre = dot(second_b, wup_ref[...])
        c0, c1 = 0.7978845608028654, 0.7978845608028654 * 0.044715
        sq = pre * pre
        tanh = jnp.tanh(pre * (c0 + c1 * sq))
        half = 0.5 + 0.5 * tanh
        hidden = (pre * half).astype(BF16)
        slope = half + half * (1.0 - tanh) * pre * (c0 + (3.0 * c1) * sq)
        upd_ref[rows, :] = (resid + dot(hidden, wdown_ref[...])).astype(BF16)
        upt = jnp.transpose(up.astype(F32)).astype(BF16)
        ddown_ref[...] += dot(upt, hidden)
        d_pre = (slope * dot(up, wdown_ref[...], 1, 1)).astype(BF16)
        dup_ref[...] += dot(jnp.transpose(second).astype(BF16), d_pre)
        d_norm = dot(d_pre, wup_ref[...], 1, 1)
        d_in, d_gain = norm_back(unit, rscale, g2, d_norm)
        dres_s[rows, :] = d_in + up.astype(F32)
        dgain_ref[1:2] += d_gain
        return carry

    lax.fori_loop(0, TOKENS // chunk, feed_forward, 0)

    def backward(zone, carry):
        for side in range(2):
            w = zone * 2 + side
            rows = pl.ds(pl.multiple_of(w * PLACES, PLACES), PLACES)
            d_win = dres_s[rows, :].astype(BF16)
            dproj_ref[...] += dot(mrg_s[w], d_win)
            d_merged = dot(wproj_ref[...], d_win, 1, 1)
            for h in range(HEADS):
                at_q = slice(h * WIDTH, (h + 1) * WIDTH)
                at_k = slice(CH + h * WIDTH, CH + (h + 1) * WIDTH)
                at_v = slice(2 * CH + h * WIDTH, 2 * CH + (h + 1) * WIDTH)
                weights = soft_s[w * HEADS + h]
                inv = inv_s[w, h : h + 1]
                d_m = d_merged[h * WIDTH : (h + 1) * WIDTH] * inv
                lean = jnp.sum(d_m * mrg_s[w, at_q].astype(F32), axis=0, keepdims=True)
                d_mb = d_m.astype(BF16)
                d_chances = dot(trip_s[w, at_v], d_mb, 0, 0)
                d_scores = weights.astype(F32) * (d_chances - lean)
                at = pl.ds(pl.multiple_of((zone * HEADS + h) * PLACES, PLACES), PLACES)
                if side == 0:
                    ds_ref[0, at, :] = d_scores[:, 0:128]
                    ds_ref[1, at, 0:16] = d_scores[:, 128:PLACES]
                else:
                    ds_ref[0, at, :] += d_scores[:, 0:128]
                    ds_ref[1, at, 0:16] += d_scores[:, 128:PLACES]
                scaled = d_scores.astype(BF16)
                dtrip_s[at_q] = (dot(trip_s[w, at_k], scaled) * SCALE).astype(BF16)
                dtrip_s[at_k] = (dot(trip_s[w, at_q], scaled, 1, 1) * (1 / LOG2E)).astype(BF16)
                dtrip_s[at_v] = dot(d_mb, weights, 1, 1).astype(BF16)
            first_t = jnp.transpose(first_s[rows, :].astype(F32)).astype(BF16)
            d_triple = dtrip_s[...]
            dqkv_ref[...] += dot(first_t, d_triple, 1, 1)
            d_first = dot(d_triple, wqkvt_s[...], 0, 0).astype(BF16).astype(F32)
            unit, rscale = normed(xw_ref[rows, :].astype(F32))
            d_in, d_gain = norm_back(unit, rscale, g1, d_first)
            dtok_ref[rows, :] = (dres_s[rows, :] + d_in).astype(BF16)
            dgain_ref[0:1] += d_gain
        return carry

    lax.fori_loop(0, ZONES, backward, 0)
    for ref in (dgain_ref, dqkv_ref, dproj_ref, dup_ref, ddown_ref):
        ref[...] = ref[...] * grad_scale


VMEM_SPEC = pl.BlockSpec(memory_space=pltpu.VMEM)
LIMIT = 56 * 1024 * 1024


def vm(shape, dtype):
    return pltpu.VMEM(shape, dtype)


def bias_of(last, table, index_table):
    return pl.pallas_call(
        gather_kernel,
        out_shape=jax.ShapeDtypeStruct((2, ROWS * PLACES, 128), F32),
        in_specs=[pl.BlockSpec(memory_space=pltpu.SMEM), VMEM_SPEC, VMEM_SPEC],
        out_specs=VMEM_SPEC,
        scratch_shapes=[vm((PLACES, 256), jnp.int32), vm((HI * ROWS, 256), F32)],
        compiler_params=pltpu.CompilerParams(vmem_limit_bytes=LIMIT),
    )(last, table, index_table)


def table_sums(d_scores, index_table):
    return pl.pallas_call(
        scatter_kernel,
        out_shape=jax.ShapeDtypeStruct((HI * ROWS, 256), F32),
        in_specs=[VMEM_SPEC, VMEM_SPEC],
        out_specs=VMEM_SPEC,
        scratch_shapes=[vm((PLACES, 256), jnp.int32), vm((HI * ROWS, 256), F32)],
        compiler_params=pltpu.CompilerParams(vmem_limit_bytes=LIMIT),
    )(d_scores, index_table)


def block_pass(grad_scale, *args):
    sd = jax.ShapeDtypeStruct
    return pl.pallas_call(
        functools.partial(main_kernel, grad_scale),
        out_shape=[
            sd((TOKENS, CH), BF16),
            sd((TOKENS, CH), BF16),
            sd((8, CH), F32),
            sd((CH, 3 * CH), F32),
            sd((CH, CH), F32),
            sd((CH, HIDDEN), F32),
            sd((CH, HIDDEN), F32),
            sd((2, ROWS * PLACES, 128), F32),
        ],
        in_specs=[VMEM_SPEC] * 9,
        out_specs=[VMEM_SPEC] * 8,
        scratch_shapes=[
            vm((3 * CH, CH), BF16),
            vm((WINDOWS * HEADS, PLACES, PLACES), BF16),
            vm((WINDOWS, 3 * CH, PLACES), BF16),
            vm((WINDOWS, CH, PLACES), BF16),
            vm((WINDOWS, 8, PLACES), F32),
            vm((TOKENS, CH), BF16),
            vm((TOKENS, CH), BF16),
            vm((TOKENS, CH), F32),
            vm((3 * CH, PLACES), BF16),
        ],
        compiler_params=pltpu.CompilerParams(vmem_limit_bytes=LIMIT),
    )(*args)


def shifted(value, axis, steps):
    count = lax.axis_size(axis)
    pairs = [(source, (source + steps) % count) for source in range(count)]
    return lax.ppermute(value, axis, pairs)


def to_windows(grid_field):
    levels, row_count, col_count, channels = grid_field.shape
    blocks = grid_field.reshape(levels // 2, 2, 6, col_count // 12, 12, channels)
    return blocks.transpose(0, 3, 1, 2, 4, 5).reshape(TOKENS, channels)


def from_windows(blocks, levels, row_count, col_count):
    blocks = blocks.reshape(4, 2, 2, 6, 12, -1)
    return blocks.transpose(0, 2, 3, 1, 4, 5).reshape(levels, row_count, col_count, -1)


def into_shifted(grid_field):
    lower_rows = shifted(grid_field[:, :3], "lat", -1)
    grid_field = jnp.concatenate([grid_field[:, 3:], lower_rows], axis=1)
    next_cols = shifted(grid_field[:, :, :6], "lon", -1)
    grid_field = jnp.concatenate([grid_field[:, :, 6:], next_cols], axis=2)
    return jnp.roll(grid_field, -1, axis=0)


def from_shifted(grid_field):
    grid_field = jnp.roll(grid_field, 1, axis=0)
    upper_rows = shifted(grid_field[:, 3:], "lat", 1)
    grid_field = jnp.concatenate([upper_rows, grid_field[:, :3]], axis=1)
    prev_cols = shifted(grid_field[:, :, 18:], "lon", 1)
    return jnp.concatenate([prev_cols, grid_field[:, :, :18]], axis=2)


def per_device(
    tokens,
    lat_valid,
    gain_attn,
    w_qkv,
    w_proj,
    gain_mlp,
    w_up,
    w_down,
    bias_table,
    index_table,
    cotangent,
):
    levels, row_count, col_count, channels = tokens.shape
    lat_count = lax.axis_size("lat")
    last = (lax.axis_index("lat") == lat_count - 1).astype(jnp.int32).reshape(1)
    grad_scale = float(levels * row_count * col_count * lat_count * lax.axis_size("lon")) ** (-0.5)
    keep_rows = (lat_valid > 0)[None, :, None, None]
    inputs = jnp.where(keep_rows, tokens, jnp.zeros_like(tokens))
    upstream = jnp.where(keep_rows, cotangent, jnp.zeros_like(cotangent))
    both = into_shifted(jnp.concatenate([inputs, upstream], axis=-1))
    bias = bias_of(last, bias_table, index_table)
    upd, dtok, d_gains, d_qkv, d_proj, d_up, d_down_t, d_scores = block_pass(
        grad_scale,
        to_windows(both[..., :CH]),
        to_windows(both[..., CH:]),
        bias,
        gain_attn.reshape(1, CH),
        w_qkv,
        w_proj,
        gain_mlp.reshape(1, CH),
        w_up,
        w_down,
    )
    sums = table_sums(d_scores, index_table) * grad_scale
    sums = sums.reshape(HI, ROWS, 256).transpose(1, 0, 2).reshape(ROWS, HI * 256)[:, :ENTRIES]
    d_table = lax.psum(sums.reshape(ZONES, HEADS, ENTRIES).astype(BF16), "lon").astype(F32)
    back = from_shifted(
        from_windows(jnp.concatenate([upd, dtok], axis=-1), levels, row_count, col_count)
    )
    back = jnp.where(keep_rows, back, jnp.zeros_like(back))
    d_gains, d_qkv, d_proj, d_up, d_down_t = lax.psum(
        (d_gains, d_qkv, d_proj, d_up, d_down_t), ("lat", "lon")
    )
    return (
        back[..., :CH],
        back[..., CH:],
        d_gains[0],
        d_qkv,
        d_proj,
        d_gains[1],
        d_up,
        d_down_t.T,
        d_table,
    )


def solution(mesh):
    field = P(None, "lat", "lon", None)
    in_specs = (field, P("lat"), P(), P(), P(), P(), P(), P(), P("lat"), P(), field)
    out_specs = (field, field, P(), P(), P(), P(), P(), P(), P("lat"))
    return jax.shard_map(
        per_device, mesh=mesh, in_specs=in_specs, out_specs=out_specs, check_vma=False
    )
```

time: 731 us -> 349 us (0.48); the launches traced: 720 us -> 348 us
  local copies, waits for them, and re-layouts: 223 us -> 18.5 us
  other arithmetic: 157 us -> 6.15 us
  matrix products: 95.9 us -> 0 us
  Pallas kernels: 0 us -> 63.2 us
  waiting for transfers between devices: 139 us -> 170 us
  starting transfers between devices: 23.5 us -> 10 us
    scatter-add x1 -> x0, other arithmetic: 113 us -> none  [table_grad(): summed = jax.ops.segment_sum(flat_scores, index_flat, num_segments=entries)]
    gather x2 -> x0, local copies, waits for them, and re-layouts: 103 us -> none  [per_device(): jnp.take(bias_table, index_flat, axis=2)]
    dot_general x66 -> x0, matrix products: 84.4 us -> none  [the longest x60 74.8 us: product(): return jnp.einsum(form, left, right, preferred_element_type=jnp.float32)]
    pallas_call x0 -> x3, Pallas kernels: none -> 63.2 us  [the longest x1 40.9 us: block_pass(): pl.pallas_call(functools.partial(main_kernel, grad_scale), out_shape=[sd(...]
    psum x2, waiting for transfers between devices: 110 us -> 163 us  [the longest x1 152 us: per_device(): lax.psum((d_gains, d_qkv, d_proj, d_up, d_down_t), ('lat', 'lon'))]
    dynamic_update_slice x28 -> x0, local copies, waits for them, and re-layouts: 27.1 us -> none  [the longest x8 14.4 us: per_device(): lax.map(zone_back, (d_incoming, windows, triple, chances, merged))]
    ppermute x12 -> x4, waiting for transfers between devices: 29.5 us -> 5.83 us  [shifted(): return lax.ppermute(value, axis, pairs)]
    add x9 -> x0, local copies, waits for them, and re-layouts: 14 us -> none  [the longest x8 13.6 us: attend(): product('bqhd,bkhd->bhqk', queries, key_part) * head_width ** (-0.5)]
  transfers between devices with their start and end apart: 14 -> 6, of which waited for: 10 -> 3; matrix products, arithmetic and copies ran while one was open for 42% -> 3% of each run, Pallas kernels for 0% -> 6%
where the time goes in v1:
time: 349 us; the launch traced here: 348 us
  waiting for transfers between devices  170 us (49%)
  blocking collectives  66.3 us (19%)
  Pallas kernels  63.2 us (18%)
  local copies, waits for them, and re-layouts  18.5 us (5%)
  between operations  14.3 us (4%)
  starting transfers between devices  10 us (3%)
  other arithmetic  6.15 us (2%)
    psum x1, waiting for transfers between devices, per_device(): lax.psum((d_gains, d_qkv, d_proj, d_up, d_down_t), ('lat', 'lon'))  152 us
    psum x1, blocking collectives, per_device(): lax.psum((d_gains, d_qkv, d_proj, d_up, d_down_t), ('lat', 'lon'))  66.3 us
    pallas_call x1, Pallas kernels, block_pass(): pl.pallas_call(functools.partial(main_kernel, grad_scale), out_shape=[sd(...  40.9 us
    pallas_call x1, Pallas kernels, bias_of(): pl.pallas_call(gather_kernel, out_shape=jax.ShapeDtypeStruct((2, ROWS * P...  11.7 us
    psum x1, waiting for transfers between devices, per_device(): lax.psum(sums.reshape(ZONES, HEADS, ENTRIES).astype(BF16), 'lon')  11 us
    unnamed x24, local copies, waits for them, and re-layouts  10.6 us
    pallas_call x1, Pallas kernels, table_sums(): pl.pallas_call(scatter_kernel, out_shape=jax.ShapeDtypeStruct((HI * ROWS,...  10.6 us
    ppermute x4, starting transfers between devices, shifted(): return lax.ppermute(value, axis, pairs)  9.95 us
  transfers between devices with their start and end apart: 6, of which 3 were waited for; matrix products, arithmetic and copies ran while one was open for 3% of the time, Pallas kernels for 6%

profile of v1, /device:TPU:0, one launch (start us, length us, event | category | flops | bytes accessed | tf_op | source)
XLA Modules:
  0.0 348.0 jit_solution(3169092415102571628)
XLA Ops:
  7.9 1.4 broadcast_select_fusion.1
  9.7 3.7 %collective-permute-start = (bf16[8,3,24,384]{3,2,1,0:T(8,128)(2,1)S(1)}, bf16[8,3,24,384]{3,2,1,0:T(8,128)(2,1)S(1)}, u32[]{:S(2)}, u32[]{:S(2)}) collective-permute-start(bf16[8,3,24,384]{3,2,1,0:T(8,128)(2,1)S(1)} %get-tuple-element.39), channel_id=1, source_target_pairs={{0,120},{8,0},{16,8},{24,16},{32,24},{40,32},{48,40},{56,48},{64,5... | collective-permute-start | bytes 1327112 | tf_op jit(solution)/shard_map/ppermute | solution.py:354
  13.4 5.8 %collective-permute-done = bf16[8,3,24,384]{3,2,1,0:T(8,128)(2,1)S(1)} collective-permute-done((bf16[8,3,24,384]{3,2,1,0:T(8,128)(2,1)S(1)}, bf16[8,3,24,384]{3,2,1,0:T(8,128)(2,1)S(1)}, u32[]{:S(2)}, u32[]{:S(2)}) %collective-permute-start) | collective-permute-done | bytes 442400 | tf_op jit(solution)/shard_map/ppermute | solution.py:354
  19.2 6.1 %collective-permute-start.1 = (bf16[8,6,6,384]{3,2,1,0:T(8,128)(2,1)S(1)}, bf16[8,6,6,384]{3,2,1,0:T(8,128)(2,1)S(1)}, u32[]{:S(2)}, u32[]{:S(2)}) collective-permute-start(bf16[8,6,6,384]{3,2,1,0:T(8,128)(2,1)S(1)} %pad_maximum_fusion.5), channel_id=1, source_target_pairs={{0,7},{1,0},{2,1},{3,2},{4,3},{5,4},{6,5},{7,6},{8,15},{9,8},{10,9... | collective-permute-start | bytes 663560 | tf_op jit(solution)/shard_map/ppermute | solution.py:354
  26.5 0.9 copy.30.wdown_ref
  27.4 0.8 copy.29.table_ref
  28.2 11.7 %shard_map.178.bias_ref = f32[2,3456,128]{2,1,0:T(8,128)} custom-call(s32[1]{0:T(128)} %bitcast.2.last_ref, f32[4,6,3312]{2,1,0:T(8,128)} %copy.29.table_ref, s32[144,144]{1,0:T(8,128)} %idx_in.3), custom_call_target="tpu_custom_call" | custom-call | tf_op jit(solution)/shard_map/pallas_call | solution.py:299
  41.4 1.1 reshape.61.cw_ref
  43.2 1.1 reshape.59.xw_ref
  44.3 40.9 %shard_map.179 = (bf16[1152,192]{1,0:T(8,128)(2,1)}, bf16[1152,192]{1,0:T(8,128)(2,1)}, f32[8,192]{1,0:T(8,128)}, f32[192,576]{1,0:T(8,128)}, f32[192,192]{1,0:T...) custom-call(bf16[1152,192]{1,0:T(8,128)(2,1)} %reshape.59.xw_ref, ...), custom_call_target="tpu_custom_call" | custom-call | tf_op jit(solution)/shard_map/pallas_call | solution.py:322
  85.2 1.6 pad_maximum_fusion.3
  88.6 10.6 %shard_map.180 = f32[312,256]{1,0:T(8,128)} custom-call(f32[2,3456,128]{2,1,0:T(8,128)} %get-tuple-element.24.ds_ref, s32[144,144]{1,0:T(8,128)} %idx_in.3), custom_call_target="tpu_custom_call" | custom-call | tf_op jit(solution)/shard_map/pallas_call | solution.py:310
  99.2 1.0 multiply_convert_fusion
  100.2 0.7 convert_element_type.8
  101.7 66.3 %psum.42 = f32[8,192]{1,0:T(8,128)S(1)} all-reduce(f32[8,192]{1,0:T(8,128)S(1)} %copy-done.4), channel_id=1, replica_groups=mesh['lat'=16,'lon'=8] {'lat','lon'}, use_global_device_ids=true, to_apply=%region_0.1 | all-reduce | flops 1536 | bytes 12288 | tf_op jit(solution)/shard_map/psum | solution.py:425
  168.8 11.0 %all-reduce.4.cloned.1.call-done = bf16[4,6,3312]{2,1,0:T(8,128)(2,1)} async-done(((bf16[4,6,3312]{2,1,0:T(8,128)(2,1)}), bf16[4,6,3312]{2,1,0:T(8,128)(2,1)}) %all-reduce.4.cloned.1.call-update) | async-done | bytes 158992 | tf_op jit(solution)/shard_map/psum | solution.py:420
  179.8 1.7 copy.35
  182.1 0.9 copy.34
  183.0 0.9 copy.33
  184.0 152.0 %all-reduce.6.cloned.1.call-done = (f32[192,576]{1,0:T(8,128)}, f32[192,192]{1,0:T(8,128)}, f32[192,768]{1,0:T(8,128)}, f32[768,192]{0,1:T(8,128)}) async-done(((f32[192,576]{1,0:T(8,128)}, f32[192,192]{1,0:T(8,128)}, f32[192,768]{1,0:T(8,128)}, f32[768,192]{0,1:T(8,128)}), (f32[192,576]{1,0:T(8,128)}, f32[192,192]{1,0:T(8,128)}, f32[192,768]{1,0:T(8,128)}, ...) | async-done | bytes 1769488 | tf_op jit(solution)/shard_map/psum | solution.py:425
  336.0 1.9 copy.43
  337.9 1.6 copy.44
  339.6 0.8 copy.45
  340.4 0.8 copy.46
  (48 shorter events, 8.1 us)
Async XLA Ops:
  7.2 172.6 %all-reduce.4.cloned.1.call-start = ((), (), s32[]{:S(2)}) async-start(), calls=%async_computation | async-start | bytes 425984 | tf_op jit(solution)/shard_map/psum | solution.py:420
  9.3 16.0 %copy-start.5 = (bf16[192]{0:T(256)(128)(2,1)S(1)}, bf16[192]{0:T(256)(128)(2,1)}, u32[]{:S(2)}) copy-start(bf16[192]{0:T(256)(128)(2,1)} %param.13) | copy-start | bytes 1156
  9.3 16.6 %copy-start.6 = (bf16[192]{0:T(256)(128)(2,1)S(1)}, bf16[192]{0:T(256)(128)(2,1)}, u32[]{:S(2)}) copy-start(bf16[192]{0:T(256)(128)(2,1)} %param.16) | copy-start | bytes 1156
  9.3 17.2 %copy-start.3 = (bf16[768,192]{0,1:T(8,128)(2,1)S(1)}, bf16[768,192]{0,1:T(8,128)(2,1)}, u32[]{:S(2)}) copy-start(bf16[768,192]{0,1:T(8,128)(2,1)} %param.18) | copy-start | bytes 884740
  9.3 18.1 %copy-start.2 = (f32[4,6,3312]{2,0,1:T(4,128)S(1)}, f32[4,6,3312]{2,0,1:T(4,128)}, u32[]{:S(2)}) copy-start(f32[4,6,3312]{2,0,1:T(4,128)} %param.19) | copy-start | bytes 953860
  9.7 9.5 %collective-permute-start = (bf16[8,3,24,384]{3,2,1,0:T(8,128)(2,1)S(1)}, bf16[8,3,24,384]{3,2,1,0:T(8,128)(2,1)S(1)}, u32[]{:S(2)}, u32[]{:S(2)}) collective-permute-start(bf16[8,3,24,384]{3,2,1,0:T(8,128)(2,1)S(1)} %get-tuple-element.39), channel_id=1, source_target_pairs={{0,120},{8,0},{16,8},{24,16},{32,24},{40,32},{48,40},{56,48},{64,5... | collective-permute-start | bytes 1327112 | tf_op jit(solution)/shard_map/ppermute | solution.py:354
  19.2 21.0 %collective-permute-start.1 = (bf16[8,6,6,384]{3,2,1,0:T(8,128)(2,1)S(1)}, bf16[8,6,6,384]{3,2,1,0:T(8,128)(2,1)S(1)}, u32[]{:S(2)}, u32[]{:S(2)}) collective-permute-start(bf16[8,6,6,384]{3,2,1,0:T(8,128)(2,1)S(1)} %pad_maximum_fusion.5), channel_id=1, source_target_pairs={{0,7},{1,0},{2,1},{3,2},{4,3},{5,4},{6,5},{7,6},{8,15},{9,8},{10,9... | collective-permute-start | bytes 663560 | tf_op jit(solution)/shard_map/ppermute | solution.py:354
  88.5 79.5 %collective-permute-start.2 = (bf16[8,3,24,384]{3,0,2,1:T(8,128)(2,1)S(1)}, bf16[8,3,24,384]{3,0,2,1:T(8,128)(2,1)S(1)}, u32[]{:S(2)}, u32[]{:S(2)}) collective-permute-start(bf16[8,3,24,384]{3,0,2,1:T(8,128)(2,1)S(1)} %fusion.4), channel_id=1, source_target_pairs={{0,8},{8,16},{16,24},{24,32},{32,40},{40,48},{48,56},{56,64},{64,7... | collective-permute-start | bytes 1327112 | tf_op jit(solution)/shard_map/ppermute | solution.py:354
  99.2 2.6 copy-start.4
  101.0 235.0 %all-reduce.6.cloned.1.call-start = ((), (), s32[]{:S(2)}) async-start(), calls=%async_computation.1 | async-start | bytes 3735552 | tf_op jit(solution)/shard_map/psum | solution.py:425
  168.1 13.4 %collective-permute-start.3 = (bf16[8,6,6,384]{3,0,2,1:T(8,128)(2,1)S(1)}, bf16[8,6,6,384]{3,0,2,1:T(8,128)(2,1)S(1)}, u32[]{:S(2)}, u32[]{:S(2)}) collective-permute-start(bf16[8,6,6,384]{3,0,2,1:T(8,128)(2,1)S(1)} %pad_maximum_fusion.6), channel_id=1, source_target_pairs={{0,1},{1,2},{2,3},{3,4},{4,5},{5,6},{6,7},{7,0},{8,9},{9,10},{10,1... | collective-permute-start | bytes 663560 | tf_op jit(solution)/shard_map/ppermute | solution.py:354
  336.0 3.6 %copy-start.1 = (f32[192,768]{1,0:T(8,128)S(1)}, f32[192,768]{1,0:T(8,128)}, u32[]{:S(2)}) copy-start(f32[192,768]{1,0:T(8,128)} %get-tuple-element.54) | copy-start | bytes 1769476
  336.0 4.4 %copy-start = (f32[768,192]{0,1:T(8,128)S(1)}, f32[768,192]{0,1:T(8,128)}, u32[]{:S(2)}) copy-start(f32[768,192]{0,1:T(8,128)} %get-tuple-element.55) | copy-start | bytes 1769476
Sparse Core Ops, SparseCore 0:
  101.1 78.6 all-reduce.3
  186.7 149.2 all-reduce.5

commit v2 on v1

--- a/solution.py
+++ b/solution.py
@@ -67,7 +67,7 @@
     return 3 * level + band
 
 
-def gather_kernel(last_ref, table_ref, idx_in, bias_ref, idx_ref, t2_ref):
+def gather_bias(last_band, table_ref, idx_in, bias_ref, idx_ref, t2_ref):
     transposed_index(idx_in, idx_ref)
     for hi in range(HI):
         wide = min(256, ENTRIES - hi * 256)
@@ -76,7 +76,6 @@
             if wide < 256:
                 part = jnp.concatenate([part, jnp.zeros((HEADS, 256 - wide), F32)], axis=1)
             t2_ref[hi * ROWS + zone * HEADS : hi * ROWS + (zone + 1) * HEADS, :] = part
-    last_band = last_ref[0]
 
     def step(group, carry):
         entries = entry_lanes(idx_ref, group)
@@ -104,31 +103,29 @@
     lax.fori_loop(0, GROUPS, step, 0)
 
 
-def scatter_kernel(ds_ref, idx_in, out_ref, idx_ref, acc_ref):
+def scatter_setup(idx_in, idx_ref, acc_ref):
     transposed_index(idx_in, idx_ref)
     acc_ref[...] = jnp.zeros_like(acc_ref)
+
+
+def scatter_step(ds_ref, idx_ref, acc_ref, group, carry):
+    entries = entry_lanes(idx_ref, group)
+    onehot = low_onehot(entries)
     lane = lax.broadcasted_iota(jnp.int32, (ROWS, 128), 1)
-
-    def step(group, carry):
-        entries = entry_lanes(idx_ref, group)
-        onehot = low_onehot(entries)
-        mains, rest = [], jnp.zeros((ROWS, 128), F32)
-        for i in range(8):
-            key = group * 8 + i
-            mains.append(ds_ref[0, pl.ds(key, ROWS, stride=PLACES), :])
-            rest_i = ds_ref[1, pl.ds(key, ROWS, stride=PLACES), :]
-            if i:
-                rest_i = pltpu.roll(rest_i, 16 * i, 1)
-            rest = jnp.where(lane // 16 == i, rest_i, rest)
-        grads = jnp.concatenate(mains + [rest], axis=1)
-        high = jnp.broadcast_to(entries >> 8, (ROWS, SPAN))
-        parts = [jnp.where(high == hi, grads, 0.0) for hi in range(HI)]
-        left = jnp.concatenate(parts, axis=0).astype(BF16)
-        acc_ref[...] += dot(left, onehot, 1, 1)
-        return carry
-
-    lax.fori_loop(0, GROUPS, step, 0)
-    out_ref[...] = acc_ref[...]
+    mains, rest = [], jnp.zeros((ROWS, 128), F32)
+    for i in range(8):
+        key = group * 8 + i
+        mains.append(ds_ref[0, pl.ds(key, ROWS, stride=PLACES), :])
+        rest_i = ds_ref[1, pl.ds(key, ROWS, stride=PLACES), :]
+        if i:
+            rest_i = pltpu.roll(rest_i, 16 * i, 1)
+        rest = jnp.where(lane // 16 == i, rest_i, rest)
+    grads = jnp.concatenate(mains + [rest], axis=1)
+    high = jnp.broadcast_to(entries >> 8, (ROWS, SPAN))
+    parts = [jnp.where(high == hi, grads, 0.0) for hi in range(HI)]
+    left = jnp.concatenate(parts, axis=0).astype(BF16)
+    acc_ref[...] += dot(left, onehot, 1, 1)
+    return carry
 
 
 def normed(values):
@@ -295,28 +292,6 @@
     return pltpu.VMEM(shape, dtype)
 
 
-def bias_of(last, table, index_table):
-    return pl.pallas_call(
-        gather_kernel,
-        out_shape=jax.ShapeDtypeStruct((2, ROWS * PLACES, 128), F32),
-        in_specs=[pl.BlockSpec(memory_space=pltpu.SMEM), VMEM_SPEC, VMEM_SPEC],
-        out_specs=VMEM_SPEC,
-        scratch_shapes=[vm((PLACES, 256), jnp.int32), vm((HI * ROWS, 256), F32)],
-        compiler_params=pltpu.CompilerParams(vmem_limit_bytes=LIMIT),
-    )(last, table, index_table)
-
-
-def table_sums(d_scores, index_table):
-    return pl.pallas_call(
-        scatter_kernel,
-        out_shape=jax.ShapeDtypeStruct((HI * ROWS, 256), F32),
-        in_specs=[VMEM_SPEC, VMEM_SPEC],
-        out_specs=VMEM_SPEC,
-        scratch_shapes=[vm((PLACES, 256), jnp.int32), vm((HI * ROWS, 256), F32)],
-        compiler_params=pltpu.CompilerParams(vmem_limit_bytes=LIMIT),
-    )(d_scores, index_table)
-
-
 def block_pass(grad_scale, *args):
     sd = jax.ShapeDtypeStruct
     return pl.pallas_call(
@@ -348,37 +323,445 @@
     )(*args)
 
 
-def shifted(value, axis, steps):
-    count = lax.axis_size(axis)
-    pairs = [(source, (source + steps) % count) for source in range(count)]
-    return lax.ppermute(value, axis, pairs)
-
-
-def to_windows(grid_field):
-    levels, row_count, col_count, channels = grid_field.shape
-    blocks = grid_field.reshape(levels // 2, 2, 6, col_count // 12, 12, channels)
-    return blocks.transpose(0, 3, 1, 2, 4, 5).reshape(TOKENS, channels)
-
-
-def from_windows(blocks, levels, row_count, col_count):
-    blocks = blocks.reshape(4, 2, 2, 6, 12, -1)
-    return blocks.transpose(0, 2, 3, 1, 4, 5).reshape(levels, row_count, col_count, -1)
-
-
-def into_shifted(grid_field):
-    lower_rows = shifted(grid_field[:, :3], "lat", -1)
-    grid_field = jnp.concatenate([grid_field[:, 3:], lower_rows], axis=1)
-    next_cols = shifted(grid_field[:, :, :6], "lon", -1)
-    grid_field = jnp.concatenate([grid_field[:, :, 6:], next_cols], axis=2)
-    return jnp.roll(grid_field, -1, axis=0)
-
-
-def from_shifted(grid_field):
-    grid_field = jnp.roll(grid_field, 1, axis=0)
-    upper_rows = shifted(grid_field[:, 3:], "lat", 1)
-    grid_field = jnp.concatenate([upper_rows, grid_field[:, :3]], axis=1)
-    prev_cols = shifted(grid_field[:, :, 18:], "lon", 1)
-    return jnp.concatenate([prev_cols, grid_field[:, :, :18]], axis=2)
+MESH = pl.DeviceIdType.MESH
+BAND_ROWS, SIDE_ROWS = 112, 48
+
+
+def remote(src, dst, send, recv, device):
+    return pltpu.make_async_remote_copy(
+        src_ref=src, dst_ref=dst, send_sem=send, recv_sem=recv, device_id=device, device_id_type=MESH
+    )
+
+
+def places():
+    lat, lon = lax.axis_index("lat"), lax.axis_index("lon")
+    up, down = lax.rem(lat + 1, 16), lax.rem(lat + 15, 16)
+    right, left = lax.rem(lon + 1, 8), lax.rem(lon + 7, 8)
+    after = [(up, lon), (lat, right), (up, right)]
+    before = [(down, lon), (lat, left), (down, left)]
+    return after, before
+
+
+def greet(devices):
+    barrier = pltpu.get_barrier_semaphore()
+    for device in devices:
+        pl.semaphore_signal(barrier, inc=1, device_id=device, device_id_type=MESH)
+    pl.semaphore_wait(barrier, len(devices))
+
+
+def cut_pieces(fields, valid, win, band, side, corner):
+    def zone_step(zone, carry):
+        for f, field in enumerate(fields):
+            for depth in range(2):
+                level = lax.rem(2 * zone + depth + 1, 8)
+                for i in range(6):
+                    row = field[level, i].astype(F32) * valid[i]
+                    if i < 3:
+                        at = depth * 3 + i
+                        band[f, zone, at * 18 : at * 18 + 18] = row[6:24]
+                        corner[f, zone, at * 6 : at * 6 + 6] = row[0:6]
+                    else:
+                        at = depth * 3 + i - 3
+                        side[f, zone, at * 6 : at * 6 + 6] = row[0:6]
+                        at = (depth * 6 + i - 3) * 12
+                        win[f, 2 * zone, at : at + 12] = row[6:18]
+                        win[f, 2 * zone + 1, at : at + 6] = row[18:24]
+        return carry
+
+    lax.fori_loop(0, ZONES, zone_step, 0)
+
+
+def add_pieces(win, band, side, corner):
+    def zone_step(zone, carry):
+        for f in range(2):
+            band_v = band[f, zone].astype(F32)
+            side_v = side[f, zone].astype(F32)
+            corner_v = corner[f, zone].astype(F32)
+            for depth in range(2):
+                for i in range(3):
+                    piece = depth * 3 + i
+                    at = (depth * 6 + i) * 12
+                    win[f, 2 * zone + 1, at + 6 : at + 12] = side_v[piece * 6 : piece * 6 + 6]
+                    at = (depth * 6 + i + 3) * 12
+                    win[f, 2 * zone, at : at + 12] = band_v[piece * 18 : piece * 18 + 12]
+                    win[f, 2 * zone + 1, at : at + 6] = band_v[piece * 18 + 12 : piece * 18 + 18]
+                    win[f, 2 * zone + 1, at + 6 : at + 12] = corner_v[piece * 6 : piece * 6 + 6]
+        return carry
+
+    lax.fori_loop(0, ZONES, zone_step, 0)
+
+
+def cut_back(fields, grid, band, side, corner):
+    def zone_step(zone, carry):
+        for f, field in enumerate(fields):
+            near = field[2 * zone].astype(F32)
+            far = field[2 * zone + 1].astype(F32)
+            for depth in range(2):
+                level = lax.rem(2 * zone + depth + 1, 8)
+                for i in range(6):
+                    at = (depth * 6 + i) * 12
+                    left, mid, right = near[at : at + 12], far[at : at + 6], far[at + 6 : at + 12]
+                    if i < 3:
+                        piece = depth * 3 + i
+                        grid[f, level, i + 3, 6:18] = left
+                        grid[f, level, i + 3, 18:24] = mid
+                        side[f, zone, piece * 6 : piece * 6 + 6] = right
+                    else:
+                        piece = depth * 3 + i - 3
+                        band[f, zone, piece * 18 : piece * 18 + 12] = left
+                        band[f, zone, piece * 18 + 12 : piece * 18 + 18] = mid
+                        corner[f, zone, piece * 6 : piece * 6 + 6] = right
+        return carry
+
+    lax.fori_loop(0, ZONES, zone_step, 0)
+
+
+def add_back(grid, band, side, corner):
+    def zone_step(zone, carry):
+        for f in range(2):
+            band_v = band[f, zone].astype(F32)
+            side_v = side[f, zone].astype(F32)
+            corner_v = corner[f, zone].astype(F32)
+            for depth in range(2):
+                level = lax.rem(2 * zone + depth + 1, 8)
+                for i in range(3):
+                    piece = depth * 3 + i
+                    grid[f, level, i, 6:24] = band_v[piece * 18 : piece * 18 + 18]
+                    grid[f, level, i, 0:6] = corner_v[piece * 6 : piece * 6 + 6]
+                    grid[f, level, i + 3, 0:6] = side_v[piece * 6 : piece * 6 + 6]
+        return carry
+
+    lax.fori_loop(0, ZONES, zone_step, 0)
+
+
+def piece_scratch():
+    out = []
+    for kind in (F32, BF16, BF16):
+        for rows in (BAND_ROWS, SIDE_ROWS, SIDE_ROWS):
+            out.append(vm((2, ZONES, rows, CH), kind))
+    return out
+
+
+def clear(refs):
+    for ref in refs:
+        ref[...] = jnp.zeros_like(ref)
+
+
+def shift_in_kernel(
+    valid_ref, tok_ref, cot_ref, table_ref, idx_in, xw_ref, cw_ref, bias_ref, idx_ref, t2_ref, win,
+    band, side, corner, band_s, side_s, corner_s, band_r, side_r, corner_r, sems,
+):
+    after, before = places()
+    clear((band, side, corner))
+    valid = [valid_ref[i].astype(F32) for i in range(6)]
+    cut_pieces((tok_ref, cot_ref), valid, win, band, side, corner)
+    for source, target in ((band, band_s), (side, side_s), (corner, corner_s)):
+        target[...] = source[...].astype(BF16)
+    greet(after + before)
+    pairs = ((band_s, band_r), (side_s, side_r), (corner_s, corner_r))
+    copies = [
+        remote(src, dst, sems.at[0, i], sems.at[1, i], before[i])
+        for i, (src, dst) in enumerate(pairs)
+    ]
+    for copy in copies:
+        copy.start()
+    last_band = (lax.axis_index("lat") == 15).astype(jnp.int32)
+    gather_bias(last_band, table_ref, idx_in, bias_ref, idx_ref, t2_ref)
+    for copy in copies:
+        copy.wait()
+    add_pieces(win, band_r, side_r, corner_r)
+    xw_ref[...] = win[0].reshape(TOKENS, CH).astype(BF16)
+    cw_ref[...] = win[1].reshape(TOKENS, CH).astype(BF16)
+
+
+def shift_in(valid, tokens, cotangent, table, index_table):
+    sd = jax.ShapeDtypeStruct
+    return pl.pallas_call(
+        shift_in_kernel,
+        out_shape=[
+            sd((TOKENS, CH), BF16),
+            sd((TOKENS, CH), BF16),
+            sd((2, ROWS * PLACES, 128), F32),
+        ],
+        in_specs=[pl.BlockSpec(memory_space=pltpu.SMEM)] + [VMEM_SPEC] * 4,
+        out_specs=[VMEM_SPEC] * 3,
+        scratch_shapes=[
+            vm((PLACES, 256), jnp.int32),
+            vm((HI * ROWS, 256), F32),
+            vm((2, WINDOWS, PLACES, CH), F32),
+            *piece_scratch(),
+            pltpu.SemaphoreType.DMA((2, 3)),
+        ],
+        compiler_params=pltpu.CompilerParams(
+            vmem_limit_bytes=LIMIT, collective_id=0, has_side_effects=True
+        ),
+    )(valid, tokens, cotangent, table, index_table)
+
+
+TILES = 224
+HALF = 112
+STREAMS = ((0, 4), (64, 3))
+
+
+def reduce_kernel(
+    grad_scale, valid_ref, upd_ref, dtok_ref, dgain_ref, dqkv_ref, dproj_ref, dup_ref, ddown_ref,
+    ds_ref, idx_in,
+    updo_ref, dtoko_ref, gain_ref, qkvo_ref, projo_ref, upo_ref, downo_ref, table_ref,
+    idx_ref, acc_ref, grid, band, side, corner, band_s, side_s, corner_s, band_r, side_r, corner_r,
+    part, core_r, first_r, second_r, depth_r, full, tab_s, tab_r, tab_full,
+    halo_sems, core_sems, first_sems, second_sems, depth_sems, tab_sems,
+):
+    lat, lon = lax.axis_index("lat"), lax.axis_index("lon")
+    core, x, z_lo = lat % 2, lat // 2 % 4, lat // 8
+    y, z_hi = lon % 4, lon // 4
+    z = z_hi * 2 + z_lo
+
+    def device(core=core, x=x, y=y, z=z):
+        return (z % 2 * 4 + x) * 2 + core, z // 2 * 4 + y
+
+    sibling = device(core=1 - core)
+    along_x = [device(x=lax.rem(x + d, 4)) for d in range(1, 4)]
+    along_y = [device(y=lax.rem(y + d, 4)) for d in range(1, 4)]
+    along_z = [device(z=lax.rem(z + d, 4)) for d in range(1, 4)]
+    along_lon = [(lat, lax.rem(lon + d, 8)) for d in range(1, 8)]
+    after, before = places()
+    greet([sibling] + along_x + along_y + along_z + along_lon + after + before)
+
+    def put(tile, value):
+        part[tile : tile + 12] = value.astype(BF16).reshape(12, 16, 128)
+
+    for i in range(6):
+        put(12 * i, dup_ref[:, 128 * i : 128 * i + 128])
+        put(72 + 12 * i, ddown_ref[:, 128 * i : 128 * i + 128])
+    for i in range(4):
+        put(144 + 12 * i, dqkv_ref[:, 128 * i : 128 * i + 128])
+    put(192, jnp.concatenate([dqkv_ref[:, 512:576], dproj_ref[:, 0:64]], axis=1))
+    put(204, dproj_ref[:, 64:192])
+    gains = jnp.concatenate([dgain_ref[:, 128:192], jnp.zeros((8, 64), F32)], axis=1)
+    part[216] = jnp.concatenate([dgain_ref[:, 0:128], gains], axis=0).astype(BF16)
+    part[217:TILES] = jnp.zeros((TILES - 217, 16, 128), BF16)
+
+    mine = core * HALF
+    core_copy = remote(
+        part.at[pl.ds((1 - core) * HALF, HALF)], core_r, core_sems.at[0], core_sems.at[1], sibling
+    )
+    core_copy.start()
+
+    clear((band, side, corner))
+    cut_back((upd_ref, dtok_ref), grid, band, side, corner)
+    for source, target in ((band, band_s), (side, side_s), (corner, corner_s)):
+        target[...] = source[...].astype(BF16)
+    pairs = ((band_s, band_r), (side_s, side_r), (corner_s, corner_r))
+    halo = [
+        remote(src, dst, halo_sems.at[0, i], halo_sems.at[1, i], after[i])
+        for i, (src, dst) in enumerate(pairs)
+    ]
+
+    core_copy.wait()
+    half = pl.ds(mine, HALF)
+    part[half] = (part[half].astype(F32) + core_r[...].astype(F32)).astype(BF16)
+
+    orders = ((along_x, x, along_y, y), (along_y, y, along_x, x))
+
+    def scatter_phase(level, received, sems, starts, counts):
+        copies = []
+        for s in range(2):
+            partners, me = orders[s][2 * level], orders[s][2 * level + 1]
+            for d in range(1, 4):
+                there = lax.rem(me + d, 4)
+                source = part.at[pl.ds(starts[s] + there * counts[s], counts[s])]
+                target = received[s].at[d - 1]
+                copy = remote(
+                    source, target, sems.at[0, s, d - 1], sems.at[1, s, d - 1], partners[d - 1]
+                )
+                copy.start()
+                copies.append(copy)
+        return copies
+
+    def sum_phase(level, received, starts, counts):
+        out = []
+        for s in range(2):
+            at = starts[s] + orders[s][2 * level + 1] * counts[s]
+            own = pl.ds(at, counts[s])
+            total = part[own].astype(F32)
+            for d in range(3):
+                total += received[s][d].astype(F32)
+            part[own] = total.astype(BF16)
+            out.append(at)
+        return out
+
+    starts = [mine + STREAMS[s][0] for s in range(2)]
+    wide = [4 * STREAMS[s][1] for s in range(2)]
+    narrow = [STREAMS[s][1] for s in range(2)]
+    copies = scatter_phase(0, first_r, first_sems, starts, wide)
+    for copy in halo:
+        copy.start()
+
+    scatter_setup(idx_in, idx_ref, acc_ref)
+    lax.fori_loop(0, 9, functools.partial(scatter_step, ds_ref, idx_ref, acc_ref), 0)
+
+    for copy in copies:
+        copy.wait()
+    starts1 = sum_phase(0, first_r, starts, wide)
+    copies = scatter_phase(1, second_r, second_sems, starts1, narrow)
+
+    lax.fori_loop(9, GROUPS, functools.partial(scatter_step, ds_ref, idx_ref, acc_ref), 0)
+    tab_s[...] = jnp.zeros_like(tab_s)
+    for hi in range(0, HI, 2):
+        rows = min(48, (HI - hi) * ROWS)
+        tab_s[hi // 2, 0:rows] = (acc_ref[hi * ROWS : hi * ROWS + rows] * grad_scale).astype(BF16)
+    tab_copies = []
+    for d in range(1, 8):
+        copy = remote(
+            tab_s.at[lax.rem(lon + d, 8)],
+            tab_r.at[d - 1],
+            tab_sems.at[0, d - 1],
+            tab_sems.at[1, d - 1],
+            along_lon[d - 1],
+        )
+        copy.start()
+        tab_copies.append(copy)
+
+    for copy in copies:
+        copy.wait()
+    starts2 = sum_phase(1, second_r, starts1, narrow)
+
+    copies = []
+    for s in range(2):
+        depth_r[s][pl.ds(z, 1)] = part[pl.ds(starts2[s], narrow[s])][None]
+    for s in range(2):
+        for d in range(1, 4):
+            copy = remote(
+                part.at[pl.ds(starts2[s], narrow[s])],
+                depth_r[s].at[z],
+                depth_sems.at[0, s, d - 1],
+                depth_sems.at[1, s, d - 1],
+                along_z[d - 1],
+            )
+            copy.start()
+            copies.append(copy)
+    for copy in tab_copies:
+        copy.wait()
+    total = tab_s[lon].astype(F32)
+    for d in range(7):
+        total += tab_r[d].astype(F32)
+    tab_full[lon] = total.astype(BF16)
+    tab_copies = []
+    for d in range(1, 8):
+        copy = remote(
+            tab_full.at[lon],
+            tab_full.at[lon],
+            tab_sems.at[2, d - 1],
+            tab_sems.at[3, d - 1],
+            along_lon[d - 1],
+        )
+        copy.start()
+        tab_copies.append(copy)
+    for copy in copies:
+        copy.wait()
+    for s in range(2):
+        total = depth_r[s][0].astype(F32)
+        for d in range(1, 4):
+            total += depth_r[s][d].astype(F32)
+        full[pl.ds(starts2[s], narrow[s])] = total.astype(BF16)
+
+    def gather_phase(level, sems, begin, counts):
+        copies = []
+        for s in range(2):
+            partners = orders[s][2 * level]
+            for d in range(1, 4):
+                region = full.at[pl.ds(begin[s], counts[s])]
+                copy = remote(
+                    region, region, sems.at[2, s, d - 1], sems.at[3, s, d - 1], partners[d - 1]
+                )
+                copy.start()
+                copies.append(copy)
+        return copies
+
+    copies = gather_phase(1, second_sems, starts2, narrow)
+    for copy in halo:
+        copy.wait()
+    add_back(grid, band_r, side_r, corner_r)
+    for copy in copies:
+        copy.wait()
+    copies = gather_phase(0, first_sems, starts1, wide)
+    for i in range(6):
+        valid = valid_ref[i].astype(F32)
+        updo_ref[:, i] = (grid[0, :, i] * valid).astype(BF16)
+        dtoko_ref[:, i] = (grid[1, :, i] * valid).astype(BF16)
+    for copy in copies:
+        copy.wait()
+    region = full.at[pl.ds(mine, HALF)]
+    core_copy = remote(region, region, core_sems.at[2], core_sems.at[3], sibling)
+    core_copy.start()
+    for copy in tab_copies:
+        copy.wait()
+    for hi in range(HI):
+        wide_hi = min(256, ENTRIES - hi * 256)
+        block = tab_full[hi // 2].astype(F32)[hi % 2 * ROWS : (hi % 2 + 1) * ROWS]
+        for zone in range(ZONES):
+            table_ref[zone, :, hi * 256 : hi * 256 + wide_hi] = block[
+                zone * HEADS : (zone + 1) * HEADS, 0:wide_hi
+            ]
+    core_copy.wait()
+
+    def get(tile):
+        return full[tile : tile + 12].reshape(192, 128).astype(F32)
+
+    for i in range(6):
+        upo_ref[:, 128 * i : 128 * i + 128] = get(12 * i)
+        downo_ref[128 * i : 128 * i + 128, :] = jnp.transpose(get(72 + 12 * i))
+    for i in range(4):
+        qkvo_ref[:, 128 * i : 128 * i + 128] = get(144 + 12 * i)
+    mixed = get(192)
+    qkvo_ref[:, 512:576] = mixed[:, 0:64]
+    projo_ref[...] = jnp.concatenate([mixed[:, 64:128], get(204)], axis=1)
+    gains = full[216].astype(F32)
+    gain_ref[...] = jnp.concatenate([gains[0:8], gains[8:16, 0:64]], axis=1)
+
+
+def reduce_all(grad_scale, *args):
+    sd = jax.ShapeDtypeStruct
+    sem = pltpu.SemaphoreType.DMA
+    return pl.pallas_call(
+        functools.partial(reduce_kernel, grad_scale),
+        out_shape=[
+            sd((8, 6, 24, CH), BF16),
+            sd((8, 6, 24, CH), BF16),
+            sd((8, CH), F32),
+            sd((CH, 3 * CH), F32),
+            sd((CH, CH), F32),
+            sd((CH, HIDDEN), F32),
+            sd((HIDDEN, CH), F32),
+            sd((ZONES, HEADS, ENTRIES), F32),
+        ],
+        in_specs=[pl.BlockSpec(memory_space=pltpu.SMEM)] + [VMEM_SPEC] * 9,
+        out_specs=[VMEM_SPEC] * 8,
+        scratch_shapes=[
+            vm((PLACES, 256), jnp.int32),
+            vm((HI * ROWS, 256), F32),
+            vm((2, 8, 6, 24, CH), F32),
+            *piece_scratch(),
+            vm((TILES, 16, 128), BF16),
+            vm((HALF, 16, 128), BF16),
+            [vm((3, 4 * n, 16, 128), BF16) for _, n in STREAMS],
+            [vm((3, n, 16, 128), BF16) for _, n in STREAMS],
+            [vm((4, n, 16, 128), BF16) for _, n in STREAMS],
+            vm((TILES, 16, 128), BF16),
+            vm((8, 48, 256), BF16),
+            vm((7, 48, 256), BF16),
+            vm((8, 48, 256), BF16),
+            sem((2, 3)),
+            sem((4,)),
+            sem((4, 2, 3)),
+            sem((4, 2, 3)),
+            sem((2, 2, 3)),
+            sem((4, 7)),
+        ],
+        compiler_params=pltpu.CompilerParams(
+            vmem_limit_bytes=LIMIT, collective_id=1, has_side_effects=True
+        ),
+    )(*args)
 
 
 def per_device(
@@ -395,18 +778,12 @@
     cotangent,
 ):
     levels, row_count, col_count, channels = tokens.shape
-    lat_count = lax.axis_size("lat")
-    last = (lax.axis_index("lat") == lat_count - 1).astype(jnp.int32).reshape(1)
-    grad_scale = float(levels * row_count * col_count * lat_count * lax.axis_size("lon")) ** (-0.5)
-    keep_rows = (lat_valid > 0)[None, :, None, None]
-    inputs = jnp.where(keep_rows, tokens, jnp.zeros_like(tokens))
-    upstream = jnp.where(keep_rows, cotangent, jnp.zeros_like(cotangent))
-    both = into_shifted(jnp.concatenate([inputs, upstream], axis=-1))
-    bias = bias_of(last, bias_table, index_table)
+    grad_scale = float(levels * row_count * col_count * 128) ** (-0.5)
+    xw, cw, bias = shift_in(lat_valid, tokens, cotangent, bias_table, index_table)
     upd, dtok, d_gains, d_qkv, d_proj, d_up, d_down_t, d_scores = block_pass(
         grad_scale,
-        to_windows(both[..., :CH]),
-        to_windows(both[..., CH:]),
+        xw,
+        cw,
         bias,
         gain_attn.reshape(1, CH),
         w_qkv,
@@ -415,27 +792,20 @@
         w_up,
         w_down,
     )
-    sums = table_sums(d_scores, index_table) * grad_scale
-    sums = sums.reshape(HI, ROWS, 256).transpose(1, 0, 2).reshape(ROWS, HI * 256)[:, :ENTRIES]
-    d_table = lax.psum(sums.reshape(ZONES, HEADS, ENTRIES).astype(BF16), "lon").astype(F32)
-    back = from_shifted(
-        from_windows(jnp.concatenate([upd, dtok], axis=-1), levels, row_count, col_count)
-    )
-    back = jnp.where(keep_rows, back, jnp.zeros_like(back))
-    d_gains, d_qkv, d_proj, d_up, d_down_t = lax.psum(
-        (d_gains, d_qkv, d_proj, d_up, d_down_t), ("lat", "lon")
-    )
-    return (
-        back[..., :CH],
-        back[..., CH:],
-        d_gains[0],
+    updated, d_tokens, d_gains, d_qkv, d_proj, d_up, d_down, d_table = reduce_all(
+        grad_scale,
+        lat_valid,
+        upd.reshape(WINDOWS, PLACES, CH),
+        dtok.reshape(WINDOWS, PLACES, CH),
+        d_gains,
         d_qkv,
         d_proj,
-        d_gains[1],
         d_up,
-        d_down_t.T,
-        d_table,
+        d_down_t,
+        d_scores,
+        index_table,
     )
+    return updated, d_tokens, d_gains[0], d_qkv, d_proj, d_gains[1], d_up, d_down, d_table
 
 
 def solution(mesh):

time: 349 us -> 128 us (0.37)
  waiting for transfers between devices: 170 us -> 0 us
  blocking collectives: 66.3 us -> 0 us
  Pallas kernels: 63.2 us -> 109 us
  between operations: 14.3 us -> 0.7 us
  starting transfers between devices: 10 us -> 0 us
  other arithmetic: 6.15 us -> 0 us
    psum x2 -> x0, waiting for transfers between devices: 163 us -> none  [the longest x1 152 us: per_device(): lax.psum((d_gains, d_qkv, d_proj, d_up, d_down_t), ('lat', 'lon'))]
    psum x1 -> x0, blocking collectives: 66.3 us -> none  [per_device(): lax.psum((d_gains, d_qkv, d_proj, d_up, d_down_t), ('lat', 'lon'))]
    pallas_call x2, Pallas kernels: 22.3 us -> 68.4 us  [the longest x1 46.4 us: reduce_all(): pl.pallas_call(functools.partial(reduce_kernel, grad_scale), out_shape=[s...]
    ppermute x4 -> x0, starting transfers between devices: 9.95 us -> none  [shifted(): return lax.ppermute(value, axis, pairs)]
    ppermute x4 -> x0, waiting for transfers between devices: 5.83 us -> none  [shifted(): return lax.ppermute(value, axis, pairs)]
    unnamed x24 -> x17, local copies, waits for them, and re-layouts: 10.6 us -> 12.8 us
  transfers between devices with their start and end apart: 6 -> 0, of which waited for: 3 -> 0; matrix products, arithmetic and copies ran while one was open for 3% -> 0% of each run, Pallas kernels for 6% -> 0%
where the time goes in v2:
time: 128 us; the launch traced here: 127 us
  Pallas kernels  109 us (85%)
  local copies, waits for them, and re-layouts  16.7 us (13%)
    pallas_call x1, Pallas kernels, reduce_all(): pl.pallas_call(functools.partial(reduce_kernel, grad_scale), out_shape=[s...  46.4 us
    pallas_call x1, Pallas kernels, block_pass(): pl.pallas_call(functools.partial(main_kernel, grad_scale), out_shape=[sd(...  40.8 us
    pallas_call x1, Pallas kernels, shift_in(): pl.pallas_call(shift_in_kernel, out_shape=[sd((TOKENS, CH), BF16), sd((TO...  22 us
    unnamed x17, local copies, waits for them, and re-layouts  12.8 us

profile of v2, /device:TPU:0, one launch (start us, length us, event | category | flops | bytes accessed | tf_op | source)
XLA Modules:
  0.0 126.6 jit_solution(17136903683616692692)
XLA Ops:
  0.6 1.2 reshape.30.g1_ref
  1.9 1.2 reshape.31.g2_ref
  3.1 1.9 %copy.21.wdown_ref = bf16[768,192]{1,0:T(8,128)(2,1)} copy(bf16[768,192]{0,1:T(8,128)(2,1)} %param.18) | data formatting | bytes 589824 | tf_op args[7]
  5.0 1.8 %copy.20.table_ref = f32[4,6,3312]{2,1,0:T(8,128)} copy(f32[4,6,3312]{2,0,1:T(4,128)} %param.19) | data formatting | bytes 635904 | tf_op args[8]
  6.8 22.0 %shard_map.178 = (bf16[1152,192]{1,0:T(8,128)(2,1)}, bf16[1152,192]{1,0:T(8,128)(2,1)}, f32[2,3456,128]{2,1,0:T(8,128)}) custom-call(s32[6]{0:T(128)} %valid_ref.3, bf16[8,6,24,192]{3,2,1,0:T(8,128)(2,1)} %tok_ref.1, bf16[8,6,24,192]{3,2,1,0:T(8,128)(2,1)} %cot_ref.1, f32[4,6,3312]{2,1,0:T(8,128)} %copy.20.table_ref, s32[144,144]{1,0:T(8,128)} %idx_in.3), custom_call_target="tpu_custom_call" | custom-call | tf_op jit(solution)/shard_map/pallas_call | solution.py:479
  28.8 40.8 %shard_map.179 = (bf16[1152,192]{1,0:T(8,128)(2,1)}, bf16[1152,192]{1,0:T(8,128)(2,1)}, f32[8,192]{1,0:T(8,128)}, f32[192,576]{1,0:T(8,128)}, f32[192,192]{1,0:T...) custom-call(bf16[1152,192]{1,0:T(8,128)(2,1)} %get-tuple-element.28.xw_ref, ...), custom_call_target="tpu_custom_call" | custom-call | tf_op jit(solution)/shard_map/pallas_call | solution.py:297
  69.6 46.4 %shard_map.180 = (bf16[8,6,24,192]{3,2,1,0:T(8,128)(2,1)}, bf16[8,6,24,192]{3,2,1,0:T(8,128)(2,1)}, f32[8,192]{1,0:T(8,128)}, f32[192,576]{1,0:T(8,128)}, f32[19...) custom-call(s32[6]{0:T(128)} %valid_ref.3, bf16[8,144,192]{2,1,0:T(8,128)(2,1)} %bitcast.4, ...), custom_call_target="tpu_custom_call" | custom-call | tf_op jit(solution)/shard_map/pallas_call | solution.py:726
  116.1 0.0 copy-start.1
  116.1 0.0 copy-start.2
  116.1 0.0 copy-start.3
  116.1 0.0 copy-start
  116.1 1.4 %fusion = (f32[1,192]{1,0:T(1,128)}, f32[1,192]{1,0:T(1,128)}) fusion(f32[8,192]{1,0:T(8,128)} %get-tuple-element.41), kind=kLoop, calls=%fused_computation | loop fusion | bytes 3072 | tf_op jit(solution)/shard_map/slice | solution.py:808
  117.5 1.9 %copy.23 = f32[4,6,3312]{2,0,1:T(4,128)} copy(f32[4,6,3312]{2,1,0:T(8,128)} %get-tuple-element.55) | data formatting | bytes 635904
  119.4 2.2 %copy.22 = f32[768,192]{0,1:T(8,128)} copy(f32[768,192]{1,0:T(8,128)} %get-tuple-element.54) | data formatting | bytes 1179648
  121.6 1.9 %copy.29 = bf16[8,6,24,192]{3,2,1,0:T(8,128)(2,1)} copy(bf16[8,6,24,192]{3,2,1,0:T(8,128)(2,1)} %get-tuple-element.67) | data formatting | bytes 884736
  123.5 0.0 copy-done.1
  123.5 0.8 copy.30
  124.3 0.0 copy-done.2
  124.3 0.8 copy.31
  125.1 0.0 copy-done.3
  125.1 0.7 copy.32
  125.8 0.0 copy-done
  125.8 0.8 copy.33
Async XLA Ops:
  116.1 7.4 %copy-start.1 = (bf16[8,6,24,192]{3,2,1,0:T(8,128)(2,1)S(1)}, bf16[8,6,24,192]{3,2,1,0:T(8,128)(2,1)}, u32[]{:S(2)}) copy-start(bf16[8,6,24,192]{3,2,1,0:T(8,128)(2,1)} %get-tuple-element.68) | copy-start | bytes 1327108
  116.1 8.2 %copy-start.2 = (f32[192,576]{1,0:T(8,128)S(1)}, f32[192,576]{1,0:T(8,128)}, u32[]{:S(2)}) copy-start(f32[192,576]{1,0:T(8,128)} %get-tuple-element.70) | copy-start | bytes 1327108
  116.1 9.0 %copy-start.3 = (f32[192,192]{1,0:T(8,128)S(1)}, f32[192,192]{1,0:T(8,128)}, u32[]{:S(2)}) copy-start(f32[192,192]{1,0:T(8,128)} %get-tuple-element.71) | copy-start | bytes 442372
  116.1 9.7 %copy-start = (f32[192,768]{1,0:T(8,128)S(1)}, f32[192,768]{1,0:T(8,128)}, u32[]{:S(2)}) copy-start(f32[192,768]{1,0:T(8,128)} %get-tuple-element.73) | copy-start | bytes 1769476

commit v3 on v1

v3 whole, which is shorter than its diff:
```python
import functools
import jax
import jax.numpy as jnp
from jax import lax
from jax.sharding import PartitionSpec as P
from jax.experimental import pallas as pl
from jax.experimental.pallas import tpu as pltpu

WIN_Z = 2
WIN_LAT = 6
WIN_LON = 12
PLACES = 144
HEADS = 6
WIDTH = 32
CH = 192
HIDDEN = 768
WINDOWS = 8
TOKENS = 1152
ZONES = 4
ROWS = ZONES * HEADS
ENTRIES = 3312
HI = 13
PAIRS = 7
GROUPS = 18
SPAN = 1152
LOG2E = 1.4426950408889634
SCALE = 32**-0.5
NORM_EPS = 1e-05
F32 = jnp.float32
BF16 = jnp.bfloat16


def dot(left, right, left_dim=1, right_dim=0):
    return lax.dot_general(
        left, right, (((left_dim,), (right_dim,)), ((), ())), preferred_element_type=F32
    )


def entry_lanes(idx_ref, group):
    start = pl.multiple_of(group * 8, 8)
    main = idx_ref[pl.ds(start, 8), 0:128]
    rest = idx_ref[pl.ds(start, 8), 128:256].astype(F32)
    rest = pltpu.roll(rest, 0, 1, stride=16, stride_axis=0)
    place = lax.broadcasted_iota(jnp.int32, (8, 128), 0)
    lane = lax.broadcasted_iota(jnp.int32, (8, 128), 1)
    rest = jnp.sum(jnp.where(lane // 16 == place, rest, 0.0), axis=0, keepdims=True)
    rows = [main[i : i + 1] for i in range(8)] + [rest.astype(jnp.int32)]
    return jnp.concatenate(rows, axis=1)


def low_onehot(entries):
    low = jnp.broadcast_to((entries & 255).astype(F32).astype(BF16), (256, SPAN))
    at = lax.broadcasted_iota(jnp.int32, (256, SPAN), 0).astype(F32).astype(BF16)
    return jnp.where(low == at, jnp.ones((), BF16), jnp.zeros((), BF16))


def transposed_index(idx_in, idx_ref):
    idx_ref[:, 128:256] = jnp.zeros((PLACES, 128), jnp.int32)
    idx_ref[:, 0:PLACES] = jnp.transpose(idx_in[...].astype(F32)).astype(jnp.int32)


def region_of(place, last_zone, last_band):
    depth = place // (WIN_LAT * WIN_LON)
    row = place // WIN_LON % WIN_LAT
    level = jnp.where(depth >= WIN_Z - WIN_Z // 2, 2, 1) * last_zone
    band = jnp.where(row >= WIN_LAT - WIN_LAT // 2, 2, 1) * last_band
    return 3 * level + band


def gather_bias(table_ref, idx_in, bias_ref, idx_ref, t2_ref, hot_ref):
    last_band = (lax.axis_index("lat") == 15).astype(jnp.int32)
    transposed_index(idx_in, idx_ref)
    for hi in range(HI):
        wide = min(256, ENTRIES - hi * 256)
        for head in range(HEADS):
            part = table_ref[head, :, hi * 256 : hi * 256 + wide] * LOG2E
            if wide < 256:
                part = jnp.concatenate([part, jnp.zeros((ZONES, 256 - wide), F32)], axis=1)
            t2_ref[hi * ROWS + head * ZONES : hi * ROWS + (head + 1) * ZONES, :] = part

    def step(group, carry):
        entries = entry_lanes(idx_ref, group)
        onehot = low_onehot(entries)
        hot_ref[group] = onehot
        found = dot(t2_ref[...].astype(BF16), onehot)
        high = jnp.broadcast_to(entries >> 8, (ROWS, SPAN))
        bias = jnp.where(high == 0, found[0:ROWS], 0.0)
        for hi in range(1, HI):
            bias = jnp.where(high == hi, found[hi * ROWS : (hi + 1) * ROWS], bias)
        lane = lax.broadcasted_iota(jnp.int32, (ROWS, 128), 1)
        zone3 = (lax.broadcasted_iota(jnp.int32, (ROWS, 128), 0) % ZONES == ZONES - 1).astype(
            jnp.int32
        )
        main_region = region_of(lane, zone3, last_band)
        rest_region = region_of((lane & 15) + 128, zone3, last_band)
        rest = bias[:, 1024:1152]
        for i in range(8):
            key = group * 8 + i
            key_region = region_of(jnp.full((ROWS, 128), key, jnp.int32), zone3, last_band)
            main_i = jnp.where(
                main_region == key_region, bias[:, i * 128 : (i + 1) * 128], -1e30
            )
            rest_i = rest if i == 0 else pltpu.roll(rest, 128 - 16 * i, 1)
            rest_i = jnp.where(rest_region == key_region, rest_i, -1e30)
            bias_ref[0, pl.ds(key, ROWS, stride=PLACES), :] = main_i
            bias_ref[1, pl.ds(key, ROWS, stride=PLACES), :] = rest_i
        return carry

    lax.fori_loop(0, GROUPS, step, 0)


def scatter_step(ds_ref, idx_ref, hot_ref, acc_ref, group, carry):
    entries = entry_lanes(idx_ref, group)
    lane = lax.broadcasted_iota(jnp.int32, (ROWS, 128), 1)
    mains, rest = [], jnp.zeros((ROWS, 128), F32)
    for i in range(8):
        key = group * 8 + i
        mains.append(ds_ref[0, pl.ds(key, ROWS, stride=PLACES), :])
        rest_i = ds_ref[1, pl.ds(key, ROWS, stride=PLACES), :]
        if i:
            rest_i = pltpu.roll(rest_i, 16 * i, 1)
        rest = jnp.where(lane // 16 == i, rest_i, rest)
    grads = jnp.concatenate(mains + [rest], axis=1)
    grads = jnp.concatenate([grads, grads], axis=0).astype(BF16)
    high = jnp.broadcast_to((entries >> 8).astype(F32), (ROWS, SPAN))
    high = jnp.concatenate([high, high - 1.0], axis=0).astype(BF16)
    zero = jnp.zeros((), BF16)
    parts = [jnp.where(high == jnp.full((), 2 * i, BF16), grads, zero) for i in range(PAIRS)]
    acc_ref[...] += dot(jnp.concatenate(parts, axis=0), hot_ref[group], 1, 1)
    return carry


def normed(values):
    center = values - jnp.mean(values, axis=-1, keepdims=True)
    rscale = lax.rsqrt(jnp.mean(center * center, axis=-1, keepdims=True) + NORM_EPS)
    return center * rscale, rscale


def norm_back(unit, rscale, gain, incoming):
    scaled = incoming * gain
    d_inputs = rscale * (
        scaled
        - jnp.mean(scaled, axis=-1, keepdims=True)
        - unit * jnp.mean(scaled * unit, axis=-1, keepdims=True)
    )
    return d_inputs, jnp.sum(incoming * unit, axis=0, keepdims=True)


VMEM_SPEC = pl.BlockSpec(memory_space=pltpu.VMEM)
LIMIT = 60 * 1024 * 1024


def vm(shape, dtype):
    return pltpu.VMEM(shape, dtype)


MESH = pl.DeviceIdType.MESH
BAND_ROWS, SIDE_ROWS = 112, 48


def remote(src, dst, send, recv, device):
    return pltpu.make_async_remote_copy(
        src_ref=src, dst_ref=dst, send_sem=send, recv_sem=recv, device_id=device, device_id_type=MESH
    )


def places():
    lat, lon = lax.axis_index("lat"), lax.axis_index("lon")
    up, down = lax.rem(lat + 1, 16), lax.rem(lat + 15, 16)
    right, left = lax.rem(lon + 1, 8), lax.rem(lon + 7, 8)
    after = [(up, lon), (lat, right), (up, right)]
    before = [(down, lon), (lat, left), (down, left)]
    return after, before


def cut_pieces(fields, valid, win, band, side, corner):
    def zone_step(zone, carry):
        for f, field in enumerate(fields):
            for depth in range(2):
                level = lax.rem(2 * zone + depth + 1, 8)
                for i in range(6):
                    row = field[level, i].astype(F32) * valid[i]
                    if i < 3:
                        at = depth * 3 + i
                        band[f, zone, at * 18 : at * 18 + 18] = row[6:24]
                        corner[f, zone, at * 6 : at * 6 + 6] = row[0:6]
                    else:
                        at = depth * 3 + i - 3
                        side[f, zone, at * 6 : at * 6 + 6] = row[0:6]
                        at = (depth * 6 + i - 3) * 12
                        win[f, 2 * zone, at : at + 12] = row[6:18]
                        win[f, 2 * zone + 1, at : at + 6] = row[18:24]
        return carry

    lax.fori_loop(0, ZONES, zone_step, 0)


def add_pieces(win, band, side, corner):
    def zone_step(zone, carry):
        for f in range(2):
            band_v = band[f, zone].astype(F32)
            side_v = side[f, zone].astype(F32)
            corner_v = corner[f, zone].astype(F32)
            for depth in range(2):
                for i in range(3):
                    piece = depth * 3 + i
                    at = (depth * 6 + i) * 12
                    win[f, 2 * zone + 1, at + 6 : at + 12] = side_v[piece * 6 : piece * 6 + 6]
                    at = (depth * 6 + i + 3) * 12
                    win[f, 2 * zone, at : at + 12] = band_v[piece * 18 : piece * 18 + 12]
                    win[f, 2 * zone + 1, at : at + 6] = band_v[piece * 18 + 12 : piece * 18 + 18]
                    win[f, 2 * zone + 1, at + 6 : at + 12] = corner_v[piece * 6 : piece * 6 + 6]
        return carry

    lax.fori_loop(0, ZONES, zone_step, 0)


def cut_back(field, f, grid, band, side, corner):
    def zone_step(zone, carry):
        near = field[2 * zone]
        far = field[2 * zone + 1]
        for depth in range(2):
            level = lax.rem(2 * zone + depth + 1, 8)
            for i in range(6):
                at = (depth * 6 + i) * 12
                left, mid, right = near[at : at + 12], far[at : at + 6], far[at + 6 : at + 12]
                if i < 3:
                    piece = depth * 3 + i
                    grid[f, level, i + 3, 6:18] = left
                    grid[f, level, i + 3, 18:24] = mid
                    side[f, zone, piece * 6 : piece * 6 + 6] = right
                else:
                    piece = depth * 3 + i - 3
                    band[f, zone, piece * 18 : piece * 18 + 12] = left
                    band[f, zone, piece * 18 + 12 : piece * 18 + 18] = mid
                    corner[f, zone, piece * 6 : piece * 6 + 6] = right
        return carry

    lax.fori_loop(0, ZONES, zone_step, 0)


def add_back(grid, band, side, corner):
    def zone_step(zone, carry):
        for f in range(2):
            band_v = band[f, zone].astype(F32)
            side_v = side[f, zone].astype(F32)
            corner_v = corner[f, zone].astype(F32)
            for depth in range(2):
                level = lax.rem(2 * zone + depth + 1, 8)
                for i in range(3):
                    piece = depth * 3 + i
                    grid[f, level, i, 6:24] = band_v[piece * 18 : piece * 18 + 18]
                    grid[f, level, i, 0:6] = corner_v[piece * 6 : piece * 6 + 6]
                    grid[f, level, i + 3, 0:6] = side_v[piece * 6 : piece * 6 + 6]
        return carry

    lax.fori_loop(0, ZONES, zone_step, 0)


def piece_scratch():
    out = []
    for kind in (F32, BF16, BF16, BF16, BF16):
        for rows in (BAND_ROWS, SIDE_ROWS, SIDE_ROWS):
            out.append(vm((2, ZONES, rows, CH), kind))
    return out


TILES = 224
EARLY = (0, 64, ((0, 2), (32, 2)))
LATE = (128, 48, ((0, 2), (32, 1)))


class AllReduce:
    def __init__(self, plan, part, full, spot, bufs):
        self.base, self.half, self.streams = plan
        self.part, self.full, self.spot = part, full, spot
        self.core_r, self.first_r, self.second_r, self.depth_r = bufs[:4]
        self.core_sems, self.first_sems, self.second_sems, self.depth_sems = bufs[4:]
        self.mine = self.base + spot.core * self.half
        axes = ((spot.along_x, spot.x), (spot.along_y, spot.y))
        self.orders = (axes, axes[::-1])
        self.starts = [[self.mine + first for first, _ in self.streams]]
        self.counts = [[4 * n for _, n in self.streams], [n for _, n in self.streams]]
        for level in range(2):
            self.starts.append(
                [
                    self.starts[level][s] + self.orders[s][level][1] * self.counts[level][s]
                    for s in range(2)
                ]
            )

    def core_copy(self):
        other = self.base + (1 - self.spot.core) * self.half
        source = self.part.at[pl.ds(other, self.half)]
        return remote(
            source, self.core_r, self.core_sems.at[0], self.core_sems.at[1], self.spot.sibling
        )

    def core_back(self):
        region = self.full.at[pl.ds(self.mine, self.half)]
        return remote(
            region, region, self.core_sems.at[2], self.core_sems.at[3], self.spot.sibling
        )

    def level(self, level):
        return (self.first_r, self.first_sems) if level == 0 else (self.second_r, self.second_sems)

    def scatter(self, level):
        received, sems = self.level(level)
        copies = []
        for s in range(2):
            partners, me = self.orders[s][level]
            count = self.counts[level][s]
            for d in range(3):
                at = self.starts[level][s] + lax.rem(me + d + 1, 4) * count
                source = self.part.at[pl.ds(at, count)]
                copies.append(
                    remote(
                        source, received[s].at[d], sems.at[0, s, d], sems.at[1, s, d], partners[d]
                    )
                )
        return copies

    def gather(self, level):
        _, sems = self.level(level)
        copies = []
        for s in range(2):
            region = self.full.at[pl.ds(self.starts[level + 1][s], self.counts[level][s])]
            for d in range(3):
                partner = self.orders[s][level][0][d]
                copies.append(
                    remote(region, region, sems.at[2, s, d], sems.at[3, s, d], partner)
                )
        return copies

    def depth(self):
        copies = []
        for s in range(2):
            source = self.part.at[pl.ds(self.starts[2][s], self.counts[1][s])]
            target = self.depth_r[s].at[self.spot.z]
            for d in range(3):
                sems = self.depth_sems
                copies.append(
                    remote(source, target, sems.at[0, s, d], sems.at[1, s, d], self.spot.along_z[d])
                )
        return copies

    def add(self, level):
        received, _ = self.level(level)
        for s in range(2):
            own = pl.ds(self.starts[level + 1][s], self.counts[level][s])
            total = self.part[own].astype(F32)
            for d in range(3):
                total += received[s][d].astype(F32)
            self.part[own] = total.astype(BF16)

    def step(self, number):
        if number == 0:
            self.core_copy().start()
        elif number == 1:
            self.core_copy().wait()
            own = pl.ds(self.mine, self.half)
            total = self.part[own].astype(F32) + self.core_r[...].astype(F32)
            self.part[own] = total.astype(BF16)
            start(self.scatter(0))
        elif number == 2:
            finish(self.scatter(0))
            self.add(0)
            start(self.scatter(1))
        elif number == 3:
            finish(self.scatter(1))
            self.add(1)
            for s in range(2):
                own = pl.ds(self.starts[2][s], self.counts[1][s])
                self.depth_r[s][pl.ds(self.spot.z, 1)] = self.part[own][None]
            start(self.depth())
        elif number == 4:
            finish(self.depth())
            for s in range(2):
                total = self.depth_r[s][0].astype(F32)
                for d in range(1, 4):
                    total += self.depth_r[s][d].astype(F32)
                self.full[pl.ds(self.starts[2][s], self.counts[1][s])] = total.astype(BF16)
            start(self.gather(1))
        elif number == 5:
            finish(self.gather(1))
            start(self.gather(0))
        elif number == 6:
            finish(self.gather(0))
            self.core_back().start()
        else:
            self.core_back().wait()


def all_reduce_scratch(plan):
    _, half, streams = plan
    sem = pltpu.SemaphoreType.DMA
    return [
        vm((half, 16, 128), BF16),
        [vm((3, 4 * n, 16, 128), BF16) for _, n in streams],
        [vm((3, n, 16, 128), BF16) for _, n in streams],
        [vm((4, n, 16, 128), BF16) for _, n in streams],
        sem((4,)),
        sem((4, 2, 3)),
        sem((4, 2, 3)),
        sem((2, 2, 3)),
    ]


def start(copies):
    for copy in copies:
        copy.start()


def finish(copies):
    for copy in copies:
        copy.wait()


class Spot:
    def __init__(self):
        lat, lon = lax.axis_index("lat"), lax.axis_index("lon")
        self.lat, self.lon = lat, lon
        self.core, self.x, z_lo = lat % 2, lat // 2 % 4, lat // 8
        self.y, z_hi = lon % 4, lon // 4
        self.z = z_hi * 2 + z_lo
        self.sibling = self.device(core=1 - self.core)
        self.along_x = [self.device(x=lax.rem(self.x + d, 4)) for d in range(1, 4)]
        self.along_y = [self.device(y=lax.rem(self.y + d, 4)) for d in range(1, 4)]
        self.along_z = [self.device(z=lax.rem(self.z + d, 4)) for d in range(1, 4)]
        self.along_lon = [(lat, lax.rem(lon + d, 8)) for d in range(1, 8)]
        self.after, self.before = places()
        self.all = [self.sibling] + self.along_x + self.along_y + self.along_z
        self.all += self.along_lon + self.after + self.before

    def device(self, core=None, x=None, y=None, z=None):
        core = self.core if core is None else core
        x = self.x if x is None else x
        y = self.y if y is None else y
        z = self.z if z is None else z
        return (z % 2 * 4 + x) * 2 + core, z // 2 * 4 + y


def put(part, tile, value):
    part[tile : tile + 12] = value.astype(BF16).reshape(12, 16, 128)


def block_kernel(
    grad_scale, valid_ref, tok_ref, cot_ref, table_ref, idx_in, g1_ref, wqkv_ref, wproj_ref,
    g2_ref, wup_ref, wdown_ref,
    updo_ref, dtoko_ref, full_ref, tab_ref,
    idx_ref, t2_ref, hot_ref, bias_ref, ds_ref, acc_ref, win, grid,
    band, side, corner, band_s, side_s, corner_s, band_r, side_r, corner_r,
    band_s2, side_s2, corner_s2, band_r2, side_r2, corner_r2,
    wqkvt_s, soft_s, trip_s, mrg_s, inv_s, first_s, resid_s, dres_s, dtrip_s, upd_s, dtok_s,
    dgain_s, dqkv_s, dproj_s, dup_s, ddown_s,
    part, full, early_bufs, late_bufs, tab_s, tab_r, tab_full, halo_sems, back_sems, tab_sems,
):
    spot = Spot()
    barrier = pltpu.get_barrier_semaphore()
    for device in spot.all:
        pl.semaphore_signal(barrier, inc=1, device_id=device, device_id_type=MESH)
    valid = [valid_ref[i].astype(F32) for i in range(6)]
    cut_pieces((tok_ref, cot_ref), valid, win, band, side, corner)
    for source, target in ((band, band_s), (side, side_s), (corner, corner_s)):
        target[...] = source[...].astype(BF16)
    pl.semaphore_wait(barrier, len(spot.all))
    pairs = ((band_s, band_r), (side_s, side_r), (corner_s, corner_r))
    halo = [
        remote(src, dst, halo_sems.at[0, i], halo_sems.at[1, i], spot.before[i])
        for i, (src, dst) in enumerate(pairs)
    ]
    start(halo)
    gather_bias(table_ref, idx_in, bias_ref, idx_ref, t2_ref, hot_ref)
    wqkvt_s[...] = jnp.transpose(wqkv_ref[...].astype(F32)).astype(BF16)
    g1 = g1_ref[...].astype(F32).reshape(1, CH)
    g2 = g2_ref[...].astype(F32).reshape(1, CH)
    for ref in (dgain_s, dqkv_s, dproj_s, dup_s, ddown_s, acc_ref, ds_ref):
        ref[...] = jnp.zeros_like(ref)
    finish(halo)
    add_pieces(win, band_r, side_r, corner_r)

    def forward(w, carry):
        x = win[0, w]
        first = (normed(x)[0] * g1).astype(BF16)
        first_s[w] = first
        triple = dot(wqkvt_s[...], first, 1, 1)
        trip_s[w, 0:CH] = (triple[0:CH] * (SCALE * LOG2E)).astype(BF16)
        trip_s[w, CH : 3 * CH] = triple[CH : 3 * CH].astype(BF16)
        zone = w // 2
        for h in range(HEADS):
            query = trip_s[w, h * WIDTH : (h + 1) * WIDTH]
            keys = trip_s[w, CH + h * WIDTH : CH + (h + 1) * WIDTH]
            values = trip_s[w, 2 * CH + h * WIDTH : 2 * CH + (h + 1) * WIDTH]
            at = pl.ds(pl.multiple_of((h * ZONES + zone) * PLACES, PLACES), PLACES)
            bias = jnp.concatenate([bias_ref[0, at, :], bias_ref[1, at, 0:16]], axis=1)
            scores = dot(keys, query, 0, 0) + bias
            weights = jnp.exp2(scores - jnp.max(scores, axis=0, keepdims=True))
            inv = 1.0 / jnp.sum(weights, axis=0, keepdims=True)
            weights = weights.astype(BF16)
            soft_s[w * HEADS + h] = weights
            inv_s[w, h : h + 1] = inv
            mrg_s[w, h * WIDTH : (h + 1) * WIDTH] = (dot(values, weights) * inv).astype(BF16)
        attended = dot(mrg_s[w], wproj_ref[...], 0, 0).astype(BF16).astype(F32)
        resid_s[w] = (x + attended).astype(BF16)
        return carry

    lax.fori_loop(0, WINDOWS, forward, 0)

    many = 4
    chunk = many * PLACES

    def feed_forward(c, carry):
        here = pl.ds(c * many, many)
        resid = resid_s[here].reshape(chunk, CH).astype(F32)
        up_f = win[1, here].reshape(chunk, CH)
        up = up_f.astype(BF16)
        unit, rscale = normed(resid)
        second = unit * g2
        pre = dot(second.astype(BF16), wup_ref[...])
        c0, c1 = 0.7978845608028654, 0.7978845608028654 * 0.044715
        sq = pre * pre
        tanh = jnp.tanh(pre * (c0 + c1 * sq))
        half = 0.5 + 0.5 * tanh
        hidden = (pre * half).astype(BF16)
        slope = half + half * (1.0 - tanh) * pre * (c0 + (3.0 * c1) * sq)
        upd_s[here] = (resid + dot(hidden, wdown_ref[...], 1, 1)).reshape(many, PLACES, CH)
        ddown_s[...] += dot(jnp.transpose(up_f).astype(BF16), hidden)
        d_pre = (slope * dot(up, wdown_ref[...])).astype(BF16)
        dup_s[...] += dot(jnp.transpose(second).astype(BF16), d_pre)
        d_norm = dot(d_pre, wup_ref[...], 1, 1)
        d_in, d_gain = norm_back(unit, rscale, g2, d_norm)
        dres_s[here] = (d_in + up_f).reshape(many, PLACES, CH)
        dgain_s[1:2] += d_gain
        return carry

    lax.fori_loop(0, WINDOWS // many, feed_forward, 0)

    for i in range(6):
        put(part, 12 * i, dup_s[:, 128 * i : 128 * i + 128] * grad_scale)
        put(part, 72 + 12 * i, ddown_s[:, 128 * i : 128 * i + 128] * grad_scale)
    early = AllReduce(EARLY, part, full, spot, early_bufs)
    late = AllReduce(LATE, part, full, spot, late_bufs)
    early.step(0)

    cut_back(upd_s, 0, grid, band, side, corner)
    back_pairs = ((band, band_s2, band_r2), (side, side_s2, side_r2), (corner, corner_s2, corner_r2))

    def back_copies(f):
        return [
            remote(
                src.at[f], dst.at[f], back_sems.at[0, f, i], back_sems.at[1, f, i], spot.after[i]
            )
            for i, (_, src, dst) in enumerate(back_pairs)
        ]

    for source, target, _ in back_pairs:
        target[0] = source[0].astype(BF16)
    start(back_copies(0))

    def backward(zone, carry):
        for part_of_zone in range(2):
            w = zone * 2 + part_of_zone
            d_win = dres_s[w].astype(BF16)
            dproj_s[...] += dot(mrg_s[w], d_win)
            d_merged = dot(wproj_ref[...], d_win, 1, 1)
            for h in range(HEADS):
                at_q = slice(h * WIDTH, (h + 1) * WIDTH)
                at_k = slice(CH + h * WIDTH, CH + (h + 1) * WIDTH)
                at_v = slice(2 * CH + h * WIDTH, 2 * CH + (h + 1) * WIDTH)
                weights = soft_s[w * HEADS + h]
                inv = inv_s[w, h : h + 1]
                d_m = d_merged[h * WIDTH : (h + 1) * WIDTH] * inv
                lean = jnp.sum(d_m * mrg_s[w, at_q].astype(F32), axis=0, keepdims=True)
                d_mb = d_m.astype(BF16)
                d_chances = dot(trip_s[w, at_v], d_mb, 0, 0)
                d_scores = weights.astype(F32) * (d_chances - lean)
                at = pl.ds(pl.multiple_of((h * ZONES + zone) * PLACES, PLACES), PLACES)
                ds_ref[0, at, :] += d_scores[:, 0:128]
                ds_ref[1, at, 0:16] += d_scores[:, 128:PLACES]
                scaled = d_scores.astype(BF16)
                dtrip_s[at_q] = (dot(trip_s[w, at_k], scaled) * SCALE).astype(BF16)
                dtrip_s[at_k] = (dot(trip_s[w, at_q], scaled, 1, 1) * (1 / LOG2E)).astype(BF16)
                dtrip_s[at_v] = dot(d_mb, weights, 1, 1).astype(BF16)
            first_t = jnp.transpose(first_s[w].astype(F32)).astype(BF16)
            d_triple = dtrip_s[...]
            dqkv_s[...] += dot(first_t, d_triple, 1, 1)
            d_first = dot(d_triple, wqkvt_s[...], 0, 0).astype(BF16).astype(F32)
            unit, rscale = normed(win[0, w])
            d_in, d_gain = norm_back(unit, rscale, g1, d_first)
            dtok_s[w] = dres_s[w] + d_in
            dgain_s[0:1] += d_gain
        for i in range(4):
            pl.when(zone == i)(functools.partial(early.step, i + 1))
        return carry

    lax.fori_loop(0, ZONES, backward, 0)

    for i in range(4):
        put(part, 144 + 12 * i, dqkv_s[:, 128 * i : 128 * i + 128] * grad_scale)
    mixed = jnp.concatenate([dqkv_s[:, 512:576], dproj_s[:, 0:64]], axis=1)
    put(part, 192, mixed * grad_scale)
    put(part, 204, dproj_s[:, 64:192] * grad_scale)
    gains = jnp.concatenate([dgain_s[:, 128:192], jnp.zeros((8, 64), F32)], axis=1)
    gains = jnp.concatenate([dgain_s[:, 0:128], gains], axis=0) * grad_scale
    part[216] = gains.astype(BF16)
    part[217:TILES] = jnp.zeros((TILES - 217, 16, 128), BF16)
    late.step(0)
    cut_back(dtok_s, 1, grid, band, side, corner)
    for source, target, _ in back_pairs:
        target[1] = source[1].astype(BF16)

    def scatter_groups(turn, carry):
        step = functools.partial(scatter_step, ds_ref, idx_ref, hot_ref, acc_ref)
        lax.fori_loop(turn * 3, turn * 3 + 3, step, 0)
        for i in range(6):

            def serve(i=i):
                if i < 3:
                    early.step(i + 5)
                late.step(i + 1)
                if i == 0:
                    start(back_copies(1))

            pl.when(turn == i)(serve)
        return carry

    lax.fori_loop(0, 6, scatter_groups, 0)

    lon = spot.lon
    for i in range(PAIRS):
        tab_s[i] = (acc_ref[48 * i : 48 * i + 48] * grad_scale).astype(BF16)
    tab_s[PAIRS] = jnp.zeros((48, 256), BF16)
    copies = [
        remote(
            tab_s.at[lax.rem(lon + d + 1, 8)],
            tab_r.at[d],
            tab_sems.at[0, d],
            tab_sems.at[1, d],
            spot.along_lon[d],
        )
        for d in range(7)
    ]
    start(copies)
    finish(back_copies(0))
    finish(back_copies(1))
    add_back(grid, band_r2, side_r2, corner_r2)
    finish(copies)
    total = tab_s[lon].astype(F32)
    for d in range(7):
        total += tab_r[d].astype(F32)
    tab_full[lon] = total.astype(BF16)
    copies = [
        remote(
            tab_full.at[lon],
            tab_full.at[lon],
            tab_sems.at[2, d],
            tab_sems.at[3, d],
            spot.along_lon[d],
        )
        for d in range(7)
    ]
    start(copies)
    for i in range(6):
        updo_ref[:, i] = (grid[0, :, i] * valid[i]).astype(BF16)
        dtoko_ref[:, i] = (grid[1, :, i] * valid[i]).astype(BF16)
    late.step(7)
    full_ref[...] = full[...]
    finish(copies)
    tab_ref[...] = tab_full[...]


def block_pass(grad_scale, *args):
    sd = jax.ShapeDtypeStruct
    sem = pltpu.SemaphoreType.DMA
    return pl.pallas_call(
        functools.partial(block_kernel, grad_scale),
        out_shape=[
            sd((8, 6, 24, CH), BF16),
            sd((8, 6, 24, CH), BF16),
            sd((TILES, 16, 128), BF16),
            sd((8, 48, 256), BF16),
        ],
        in_specs=[pl.BlockSpec(memory_space=pltpu.SMEM)] + [VMEM_SPEC] * 10,
        out_specs=[VMEM_SPEC] * 4,
        scratch_shapes=[
            vm((PLACES, 256), jnp.int32),
            vm((HI * ROWS, 256), F32),
            vm((GROUPS, 256, SPAN), BF16),
            vm((2, ROWS * PLACES, 128), F32),
            vm((2, ROWS * PLACES, 128), F32),
            vm((PAIRS * 48, 256), F32),
            vm((2, WINDOWS, PLACES, CH), F32),
            vm((2, 8, 6, 24, CH), F32),
            *piece_scratch(),
            vm((3 * CH, CH), BF16),
            vm((WINDOWS * HEADS, PLACES, PLACES), BF16),
            vm((WINDOWS, 3 * CH, PLACES), BF16),
            vm((WINDOWS, CH, PLACES), BF16),
            vm((WINDOWS, 8, PLACES), F32),
            vm((WINDOWS, PLACES, CH), BF16),
            vm((WINDOWS, PLACES, CH), BF16),
            vm((WINDOWS, PLACES, CH), F32),
            vm((3 * CH, PLACES), BF16),
            vm((WINDOWS, PLACES, CH), F32),
            vm((WINDOWS, PLACES, CH), F32),
            vm((8, CH), F32),
            vm((CH, 3 * CH), F32),
            vm((CH, CH), F32),
            vm((CH, HIDDEN), F32),
            vm((CH, HIDDEN), F32),
            vm((TILES, 16, 128), BF16),
            vm((TILES, 16, 128), BF16),
            all_reduce_scratch(EARLY),
            all_reduce_scratch(LATE),
            vm((8, 48, 256), BF16),
            vm((7, 48, 256), BF16),
            vm((8, 48, 256), BF16),
            sem((2, 3)),
            sem((2, 2, 3)),
            sem((4, 7)),
        ],
        compiler_params=pltpu.CompilerParams(
            vmem_limit_bytes=LIMIT, collective_id=0, has_side_effects=True
        ),
    )(*args)


def write_kernel(
    upd_ref, dtok_ref, full_ref, tab_ref,
    updo_ref, dtoko_ref, gain1_ref, qkv_ref, proj_ref, gain2_ref, up_ref, down_ref, table_ref,
):
    updo_ref[...] = upd_ref[...]
    dtoko_ref[...] = dtok_ref[...]

    def get(tile):
        return full_ref[tile : tile + 12].reshape(192, 128).astype(F32)

    for i in range(6):
        up_ref[:, 128 * i : 128 * i + 128] = get(12 * i)
        down_ref[:, 128 * i : 128 * i + 128] = get(72 + 12 * i)
    for i in range(4):
        qkv_ref[:, 128 * i : 128 * i + 128] = get(144 + 12 * i)
    mixed = get(192)
    qkv_ref[:, 512:576] = mixed[:, 0:64]
    proj_ref[...] = jnp.concatenate([mixed[:, 64:128], get(204)], axis=1)
    gains = full_ref[216].astype(F32)
    gains = jnp.concatenate([gains[0:8], gains[8:16, 0:64]], axis=1)
    gain1_ref[...] = gains[0]
    gain2_ref[...] = gains[1]
    for hi in range(HI):
        wide = min(256, ENTRIES - hi * 256)
        block = tab_ref[hi // 2].astype(F32)[hi % 2 * ROWS : (hi % 2 + 1) * ROWS]
        for head in range(HEADS):
            table_ref[head, :, hi * 256 : hi * 256 + wide] = block[
                head * ZONES : (head + 1) * ZONES, 0:wide
            ]


def write_out(*args):
    sd = jax.ShapeDtypeStruct
    return pl.pallas_call(
        write_kernel,
        out_shape=[
            sd((8, 6, 24, CH), BF16),
            sd((8, 6, 24, CH), BF16),
            sd((CH,), F32),
            sd((CH, 3 * CH), F32),
            sd((CH, CH), F32),
            sd((CH,), F32),
            sd((CH, HIDDEN), F32),
            sd((CH, HIDDEN), F32),
            sd((HEADS, ZONES, ENTRIES), F32),
        ],
        in_specs=[VMEM_SPEC] * 4,
        out_specs=[VMEM_SPEC] * 9,
        compiler_params=pltpu.CompilerParams(vmem_limit_bytes=LIMIT),
    )(*args)


def per_device(
    tokens,
    lat_valid,
    gain_attn,
    w_qkv,
    w_proj,
    gain_mlp,
    w_up,
    w_down,
    bias_table,
    index_table,
    cotangent,
):
    levels, row_count, col_count, channels = tokens.shape
    grad_scale = float(levels * row_count * col_count * 128) ** (-0.5)
    parts = block_pass(
        grad_scale,
        lat_valid,
        tokens,
        cotangent,
        bias_table.transpose(1, 0, 2),
        index_table,
        gain_attn,
        w_qkv,
        w_proj,
        gain_mlp,
        w_up,
        w_down.T,
    )
    updated, d_tokens, d_gain1, d_qkv, d_proj, d_gain2, d_up, d_down, d_table = write_out(*parts)
    d_table = d_table.transpose(1, 0, 2)
    return updated, d_tokens, d_gain1, d_qkv, d_proj, d_gain2, d_up, d_down.T, d_table


def solution(mesh):
    field = P(None, "lat", "lon", None)
    in_specs = (field, P("lat"), P(), P(), P(), P(), P(), P(), P("lat"), P(), field)
    out_specs = (field, field, P(), P(), P(), P(), P(), P(), P("lat"))
    return jax.shard_map(
        per_device, mesh=mesh, in_specs=in_specs, out_specs=out_specs, check_vma=False
    )
```

time: 349 us -> 104 us (0.30)
  waiting for transfers between devices: 170 us -> 0 us
  blocking collectives: 66.3 us -> 0 us
  Pallas kernels: 63.2 us -> 103 us
  local copies, waits for them, and re-layouts: 18.5 us -> 0 us
  between operations: 14.3 us -> 0.65 us
  starting transfers between devices: 10 us -> 0 us
  other arithmetic: 6.15 us -> 0 us
    psum x2 -> x0, waiting for transfers between devices: 163 us -> none  [the longest x1 152 us: per_device(): lax.psum((d_gains, d_qkv, d_proj, d_up, d_down_t), ('lat', 'lon'))]
    psum x1 -> x0, blocking collectives: 66.3 us -> none  [per_device(): lax.psum((d_gains, d_qkv, d_proj, d_up, d_down_t), ('lat', 'lon'))]
    pallas_call x3 -> x2, Pallas kernels: 63.2 us -> 103 us  [the longest x1 99.6 us: block_pass(): pl.pallas_call(functools.partial(block_kernel, grad_scale), out_shape=[sd...]
    unnamed x24 -> x0, local copies, waits for them, and re-layouts: 10.6 us -> none
    ppermute x4 -> x0, starting transfers between devices: 9.95 us -> none  [shifted(): return lax.ppermute(value, axis, pairs)]
    ppermute x4 -> x0, waiting for transfers between devices: 5.83 us -> none  [shifted(): return lax.ppermute(value, axis, pairs)]
    reshape x8 -> x0, local copies, waits for them, and re-layouts: 4.49 us -> none  [the longest x2 2.25 us: to_windows(): return blocks.transpose(0, 3, 1, 2, 4, 5).reshape(TOKENS, channels)]
  transfers between devices with their start and end apart: 6 -> 0, of which waited for: 3 -> 0; matrix products, arithmetic and copies ran while one was open for 3% -> 0% of each run, Pallas kernels for 6% -> 0%
where the time goes in v3:
time: 104 us
  Pallas kernels  103 us (99%)
    pallas_call x1, Pallas kernels, block_pass(): pl.pallas_call(functools.partial(block_kernel, grad_scale), out_shape=[sd...  99.6 us
    pallas_call x1, Pallas kernels, write_out(): pl.pallas_call(write_kernel, out_shape=[sd((8, 6, 24, CH), BF16), sd((8,...  3.35 us

profile of v3, /device:TPU:0, one launch (start us, length us, event | category | flops | bytes accessed | tf_op | source)
XLA Modules:
  0.0 103.6 jit_solution(15420070170335337278)
XLA Ops:
  0.6 99.6 %shard_map.178 = (bf16[8,6,24,192]{3,2,1,0:T(8,128)(2,1)}, bf16[8,6,24,192]{3,2,1,0:T(8,128)(2,1)}, bf16[224,16,128]{2,1,0:T(8,128)(2,1)}, bf16[8,48,256]{2,1,0:T(8,128)(2,1)}) custom-call(s32[6]{0:T(128)} %valid_ref.1, bf16[8,6,24,192]{3,2,1,0:T(8,128)(2,1)} %tok_ref.1, bf16[8,6,24,192]{3,2,1,0:T(8,128)(2,1)} %cot_ref.1, f32[6,4,3312]{2,1,0:T(4,128)} %bitcast.4, ...), custom_call_target="tpu_custom_call" | custom-call | tf_op jit(solution)/shard_map/pallas_call | solution.py:676
  100.3 3.3 %shard_map.179 = (bf16[8,6,24,192]{3,2,1,0:T(8,128)(2,1)}, bf16[8,6,24,192]{3,2,1,0:T(8,128)(2,1)}, f32[192]{0:T(256)}, f32[192,576]{1,0:T(8,128)}, f32[192,192]...) custom-call(bf16[8,6,24,192]{3,2,1,0:T(8,128)(2,1)} %get-tuple-element.22.upd_ref, ...), custom_call_target="tpu_custom_call" | custom-call | tf_op jit(solution)/shard_map/pallas_call | solution.py:762

commit v4 on v3

v4 whole, which is shorter than its diff:
```python
import functools
import jax
import jax.numpy as jnp
from jax import lax
from jax.sharding import PartitionSpec as P
from jax.experimental import pallas as pl
from jax.experimental.pallas import tpu as pltpu

WIN_Z = 2
WIN_LAT = 6
WIN_LON = 12
PLACES = 144
HEADS = 6
WIDTH = 32
CH = 192
HIDDEN = 768
WINDOWS = 8
TOKENS = 1152
ZONES = 4
ROWS = ZONES * HEADS
ENTRIES = 3312
HI = 13
PAIRS = 7
GROUPS = 18
SPAN = 1152
LOG2E = 1.4426950408889634
SCALE = 32**-0.5
NORM_EPS = 1e-05
F32 = jnp.float32
BF16 = jnp.bfloat16


def dot(left, right, left_dim=1, right_dim=0):
    return lax.dot_general(
        left, right, (((left_dim,), (right_dim,)), ((), ())), preferred_element_type=F32
    )


def entry_lanes(idx_ref, group):
    start = pl.multiple_of(group * 8, 8)
    main = idx_ref[pl.ds(start, 8), 0:128]
    rest = idx_ref[pl.ds(start, 8), 128:256].astype(F32)
    rest = pltpu.roll(rest, 0, 1, stride=16, stride_axis=0)
    place = lax.broadcasted_iota(jnp.int32, (8, 128), 0)
    lane = lax.broadcasted_iota(jnp.int32, (8, 128), 1)
    rest = jnp.sum(jnp.where(lane // 16 == place, rest, 0.0), axis=0, keepdims=True)
    rows = [main[i : i + 1] for i in range(8)] + [rest.astype(jnp.int32)]
    return jnp.concatenate(rows, axis=1)


def low_onehot(entries):
    low = jnp.broadcast_to((entries & 255).astype(F32).astype(BF16), (256, SPAN))
    at = lax.broadcasted_iota(jnp.int32, (256, SPAN), 0).astype(F32).astype(BF16)
    return jnp.where(low == at, jnp.ones((), BF16), jnp.zeros((), BF16))


def transposed_index(idx_in, idx_ref):
    idx_ref[:, 128:256] = jnp.zeros((PLACES, 128), jnp.int32)
    idx_ref[:, 0:PLACES] = jnp.transpose(idx_in[...].astype(F32)).astype(jnp.int32)


def region_of(place, last_zone, last_band):
    depth = place // (WIN_LAT * WIN_LON)
    row = place // WIN_LON % WIN_LAT
    level = jnp.where(depth >= WIN_Z - WIN_Z // 2, 2, 1) * last_zone
    band = jnp.where(row >= WIN_LAT - WIN_LAT // 2, 2, 1) * last_band
    return 3 * level + band


def gather_bias(table_ref, idx_in, bias_ref, idx_ref, t2_ref, hot_ref):
    last_band = (lax.axis_index("lat") == 15).astype(jnp.int32)
    transposed_index(idx_in, idx_ref)
    for hi in range(HI):
        wide = min(256, ENTRIES - hi * 256)
        for head in range(HEADS):
            part = table_ref[head, :, hi * 256 : hi * 256 + wide] * LOG2E
            if wide < 256:
                part = jnp.concatenate([part, jnp.zeros((ZONES, 256 - wide), F32)], axis=1)
            t2_ref[hi * ROWS + head * ZONES : hi * ROWS + (head + 1) * ZONES, :] = part

    def step(group, carry):
        entries = entry_lanes(idx_ref, group)
        onehot = low_onehot(entries)
        hot_ref[group] = onehot
        found = dot(t2_ref[...].astype(BF16), onehot)
        high = jnp.broadcast_to(entries >> 8, (ROWS, SPAN))
        bias = jnp.where(high == 0, found[0:ROWS], 0.0)
        for hi in range(1, HI):
            bias = jnp.where(high == hi, found[hi * ROWS : (hi + 1) * ROWS], bias)
        lane = lax.broadcasted_iota(jnp.int32, (ROWS, 128), 1)
        zone3 = (lax.broadcasted_iota(jnp.int32, (ROWS, 128), 0) % ZONES == ZONES - 1).astype(
            jnp.int32
        )
        main_region = region_of(lane, zone3, last_band)
        rest_region = region_of((lane & 15) + 128, zone3, last_band)
        rest = bias[:, 1024:1152]
        for i in range(8):
            key = group * 8 + i
            key_region = region_of(jnp.full((ROWS, 128), key, jnp.int32), zone3, last_band)
            main_i = jnp.where(
                main_region == key_region, bias[:, i * 128 : (i + 1) * 128], -1e30
            )
            rest_i = rest if i == 0 else pltpu.roll(rest, 128 - 16 * i, 1)
            rest_i = jnp.where(rest_region == key_region, rest_i, -1e30)
            bias_ref[0, pl.ds(key, ROWS, stride=PLACES), :] = main_i
            bias_ref[1, pl.ds(key, ROWS, stride=PLACES), :] = rest_i
        return carry

    lax.fori_loop(0, GROUPS, step, 0)


def scatter_step(ds_ref, idx_ref, hot_ref, acc_ref, group, carry):
    entries = entry_lanes(idx_ref, group)
    lane = lax.broadcasted_iota(jnp.int32, (ROWS, 128), 1)
    mains, rest = [], jnp.zeros((ROWS, 128), F32)
    for i in range(8):
        key = group * 8 + i
        mains.append(ds_ref[0, pl.ds(key, ROWS, stride=PLACES), :])
        rest_i = ds_ref[1, pl.ds(key, ROWS, stride=PLACES), :]
        if i:
            rest_i = pltpu.roll(rest_i, 16 * i, 1)
        rest = jnp.where(lane // 16 == i, rest_i, rest)
    grads = jnp.concatenate(mains + [rest], axis=1)
    grads = jnp.concatenate([grads, grads], axis=0).astype(BF16)
    high = jnp.broadcast_to((entries >> 8).astype(F32), (ROWS, SPAN))
    high = jnp.concatenate([high, high - 1.0], axis=0).astype(BF16)
    zero = jnp.zeros((), BF16)
    parts = [jnp.where(high == jnp.full((), 2 * i, BF16), grads, zero) for i in range(PAIRS)]
    acc_ref[...] += dot(jnp.concatenate(parts, axis=0), hot_ref[group], 1, 1)
    return carry


def normed(values):
    center = values - jnp.mean(values, axis=-1, keepdims=True)
    rscale = lax.rsqrt(jnp.mean(center * center, axis=-1, keepdims=True) + NORM_EPS)
    return center * rscale, rscale


def norm_back(unit, rscale, gain, incoming):
    scaled = incoming * gain
    d_inputs = rscale * (
        scaled
        - jnp.mean(scaled, axis=-1, keepdims=True)
        - unit * jnp.mean(scaled * unit, axis=-1, keepdims=True)
    )
    return d_inputs


VMEM_SPEC = pl.BlockSpec(memory_space=pltpu.VMEM)
LIMIT = 60 * 1024 * 1024


def vm(shape, dtype):
    return pltpu.VMEM(shape, dtype)


MESH = pl.DeviceIdType.MESH
BAND_ROWS, SIDE_ROWS = 224, 80


def remote(src, dst, send, recv, device):
    return pltpu.make_async_remote_copy(
        src_ref=src, dst_ref=dst, send_sem=send, recv_sem=recv, device_id=device, device_id_type=MESH
    )


def places():
    lat, lon = lax.axis_index("lat"), lax.axis_index("lon")
    up, down = lax.rem(lat + 1, 16), lax.rem(lat + 15, 16)
    right, left = lax.rem(lon + 1, 8), lax.rem(lon + 7, 8)
    after = [(up, lon), (lat, right), (up, right)]
    before = [(down, lon), (lat, left), (down, left)]
    return after, before


def spot_of(zone, piece, count):
    at = (zone % 2 * 6 + piece) * count
    return slice(at, at + count), slice(zone // 2 * CH, (zone // 2 + 1) * CH)


def cut_pieces(field, f, valid, win, band, side, corner):
    for zone in range(ZONES):
        for depth in range(2):
            level = (2 * zone + depth + 1) % 8
            for i in range(6):
                row = field[level, i].astype(F32) * valid[i]
                piece = depth * 3 + i % 3
                if i < 3:
                    band[f, *spot_of(zone, piece, 18)] = row[6:24]
                    corner[f, *spot_of(zone, piece, 6)] = row[0:6]
                else:
                    side[f, *spot_of(zone, piece, 6)] = row[0:6]
                    at = (depth * 6 + i - 3) * 12
                    win[f, 2 * zone, at : at + 12] = row[6:18]
                    win[f, 2 * zone + 1, at : at + 6] = row[18:24]


def add_pieces(win, band, side, corner):
    for f in range(2):
        band_v = band[f].astype(F32)
        side_v = side[f].astype(F32)
        corner_v = corner[f].astype(F32)
        for zone in range(ZONES):
            for depth in range(2):
                for i in range(3):
                    piece = depth * 3 + i
                    at = (depth * 6 + i) * 12
                    win[f, 2 * zone + 1, at + 6 : at + 12] = side_v[spot_of(zone, piece, 6)]
                    at = (depth * 6 + i + 3) * 12
                    rows = band_v[spot_of(zone, piece, 18)]
                    win[f, 2 * zone, at : at + 12] = rows[0:12]
                    win[f, 2 * zone + 1, at : at + 6] = rows[12:18]
                    win[f, 2 * zone + 1, at + 6 : at + 12] = corner_v[spot_of(zone, piece, 6)]


def cut_back(field, f, grid, band, side, corner):
    for zone in range(ZONES):
        near = field[2 * zone]
        far = field[2 * zone + 1]
        for depth in range(2):
            level = (2 * zone + depth + 1) % 8
            for i in range(6):
                at = (depth * 6 + i) * 12
                piece = depth * 3 + i % 3
                if i < 3:
                    grid[f, level, i + 3, 6:18] = near[at : at + 12]
                    grid[f, level, i + 3, 18:24] = far[at : at + 6]
                    side[f, *spot_of(zone, piece, 6)] = far[at + 6 : at + 12]
                else:
                    rows, lanes = spot_of(zone, piece, 18)
                    band[f, rows.start : rows.start + 12, lanes] = near[at : at + 12]
                    band[f, rows.start + 12 : rows.stop, lanes] = far[at : at + 6]
                    corner[f, *spot_of(zone, piece, 6)] = far[at + 6 : at + 12]


def add_back(f, grid, band, side, corner):
    band_v = band[f].astype(F32)
    side_v = side[f].astype(F32)
    corner_v = corner[f].astype(F32)
    for zone in range(ZONES):
        for depth in range(2):
            level = (2 * zone + depth + 1) % 8
            for i in range(3):
                piece = depth * 3 + i
                grid[f, level, i, 6:24] = band_v[spot_of(zone, piece, 18)]
                grid[f, level, i, 0:6] = corner_v[spot_of(zone, piece, 6)]
                grid[f, level, i + 3, 0:6] = side_v[spot_of(zone, piece, 6)]


def piece_scratch():
    out = []
    for kind in (F32, BF16, BF16, BF16, BF16):
        for rows in (BAND_ROWS, SIDE_ROWS, SIDE_ROWS):
            out.append(vm((2, rows, 2 * CH), kind))
    return out


TILES = 224
EARLY = (0, 64, 4)
LATE = (128, 48, 3)


class AllReduce:
    def __init__(self, plan, part, full, spot, bufs):
        self.base, self.half, self.count = plan
        self.part, self.full, self.spot = part, full, spot
        self.core_r, self.plane_r, self.depth_r = bufs[:3]
        self.core_sems, self.plane_sems, self.depth_sems = bufs[3:]
        self.mine = self.base + spot.core * self.half
        self.own = pl.ds(self.mine + spot.seat * self.count, self.count)

    def core_copy(self):
        other = self.base + (1 - self.spot.core) * self.half
        source = self.part.at[pl.ds(other, self.half)]
        return remote(
            source, self.core_r, self.core_sems.at[0], self.core_sems.at[1], self.spot.sibling
        )

    def core_back(self):
        region = self.full.at[pl.ds(self.mine, self.half)]
        return remote(
            region, region, self.core_sems.at[2], self.core_sems.at[3], self.spot.sibling
        )

    def scatter(self):
        copies = []
        for i, (seat, device) in enumerate(self.spot.plane):
            source = self.part.at[pl.ds(self.mine + seat * self.count, self.count)]
            sems = self.plane_sems
            copies.append(
                remote(source, self.plane_r.at[i], sems.at[0, i], sems.at[1, i], device)
            )
        return copies

    def gather(self):
        region, sems = self.full.at[self.own], self.plane_sems
        return [
            remote(region, region, sems.at[2, i], sems.at[3, i], device)
            for i, (_, device) in enumerate(self.spot.plane)
        ]

    def depth(self):
        source, sems = self.part.at[self.own], self.depth_sems
        target = self.depth_r.at[self.spot.z]
        return [
            remote(source, target, sems.at[0, d], sems.at[1, d], self.spot.along_z[d])
            for d in range(3)
        ]

    def step(self, number):
        if number == 0:
            self.core_copy().start()
        elif number == 1:
            self.core_copy().wait()
            half = pl.ds(self.mine, self.half)
            total = self.part[half].astype(F32) + self.core_r[...].astype(F32)
            self.part[half] = total.astype(BF16)
            start(self.scatter())
        elif number == 2:
            finish(self.scatter())
            total = self.part[self.own].astype(F32)
            for i in range(15):
                total += self.plane_r[i].astype(F32)
            total = total.astype(BF16)
            self.part[self.own] = total
            self.depth_r[pl.ds(self.spot.z, 1)] = total[None]
            start(self.depth())
        elif number == 3:
            finish(self.depth())
            total = self.depth_r[0].astype(F32)
            for d in range(1, 4):
                total += self.depth_r[d].astype(F32)
            self.full[self.own] = total.astype(BF16)
            start(self.gather())
        elif number == 4:
            finish(self.gather())
            self.core_back().start()
        else:
            self.core_back().wait()


def all_reduce_scratch(plan):
    _, half, count = plan
    sem = pltpu.SemaphoreType.DMA
    return [
        vm((half, 16, 128), BF16),
        vm((15, count, 16, 128), BF16),
        vm((4, count, 16, 128), BF16),
        sem((4,)),
        sem((4, 15)),
        sem((2, 3)),
    ]


def start(copies):
    for copy in copies:
        copy.start()


def finish(copies):
    for copy in copies:
        copy.wait()


class Spot:
    def __init__(self):
        lat, lon = lax.axis_index("lat"), lax.axis_index("lon")
        self.lat, self.lon = lat, lon
        self.core, self.x, z_lo = lat % 2, lat // 2 % 4, lat // 8
        self.y, z_hi = lon % 4, lon // 4
        self.z = z_hi * 2 + z_lo
        self.sibling = self.device(core=1 - self.core)
        self.seat = self.x * 4 + self.y
        self.plane = []
        for d in range(1, 16):
            x, y = lax.rem(self.x + d // 4, 4), lax.rem(self.y + d % 4, 4)
            self.plane.append((x * 4 + y, self.device(x=x, y=y)))
        self.along_z = [self.device(z=lax.rem(self.z + d, 4)) for d in range(1, 4)]
        self.along_lon = [(lat, lax.rem(lon + d, 8)) for d in range(1, 8)]
        self.after, self.before = places()
        far = [(lat, (1 - z_hi) * 4 + lax.rem(self.y + d, 4)) for d in range(1, 4)]
        self.all = [self.sibling] + [device for _, device in self.plane] + self.along_z + far
        self.all += [self.after[0], self.after[2], self.before[0], self.before[2]]

    def device(self, core=None, x=None, y=None, z=None):
        core = self.core if core is None else core
        x = self.x if x is None else x
        y = self.y if y is None else y
        z = self.z if z is None else z
        return (z % 2 * 4 + x) * 2 + core, z // 2 * 4 + y


def put(part, tile, value):
    part[tile : tile + 12] = value.astype(BF16).reshape(12, 16, 128)


def block_kernel(
    grad_scale, valid_ref, tok_ref, cot_ref, table_ref, idx_in, g1_ref, wqkv_ref, wproj_ref,
    g2_ref, wup_ref, wdown_ref,
    updo_ref, dtoko_ref, full_ref, tab_ref,
    idx_ref, t2_ref, hot_ref, bias_ref, acc_ref, win, grid,
    band, side, corner, band_s, side_s, corner_s, band_r, side_r, corner_r,
    band_s2, side_s2, corner_s2, band_r2, side_r2, corner_r2,
    wqkvt_s, soft_s, trip_s, mrg_s, inv_s, first_s, resid_s, dres_s, dtrip_s, dsoft_s, dmrg_s, upd_s,
    dqkv_s, dproj_s, dup_s, ddown_s,
    part, full, early_bufs, late_bufs, tab_s, tab_r, tab_full, halo_sems, back_sems, tab_sems,
):
    ds_ref = bias_ref
    spot = Spot()
    barrier = pltpu.get_barrier_semaphore()
    for device in spot.all:
        pl.semaphore_signal(barrier, inc=1, device_id=device, device_id_type=MESH)
    valid = [valid_ref[i].astype(F32) for i in range(6)]
    cut_pieces(tok_ref, 0, valid, win, band, side, corner)
    cut_pieces(cot_ref, 1, valid, win, band, side, corner)
    for source, target in ((band, band_s), (side, side_s), (corner, corner_s)):
        target[...] = source[...].astype(BF16)
    pl.semaphore_wait(barrier, len(spot.all))
    pairs = ((band_s, band_r), (side_s, side_r), (corner_s, corner_r))
    halo = [
        remote(src, dst, halo_sems.at[0, i], halo_sems.at[1, i], spot.before[i])
        for i, (src, dst) in enumerate(pairs)
    ]
    start(halo)
    gather_bias(table_ref, idx_in, bias_ref, idx_ref, t2_ref, hot_ref)
    wqkvt_s[...] = jnp.transpose(wqkv_ref[...].astype(F32)).astype(BF16)
    g1 = g1_ref[...].astype(F32).reshape(1, CH)
    g2 = g2_ref[...].astype(F32).reshape(1, CH)
    for ref in (dqkv_s, dproj_s, dup_s, ddown_s, acc_ref):
        ref[...] = jnp.zeros_like(ref)
    finish(halo)
    add_pieces(win, band_r, side_r, corner_r)

    def forward(zone, carry):
        windows = [zone * 2, zone * 2 + 1]
        triples, scores, softs = [], [], []
        for w in windows:
            first = (normed(win[0, w])[0] * g1).astype(BF16)
            first_s[w] = first
            triple = dot(wqkvt_s[...], first, 1, 1)
            queries = (triple[0:CH] * (SCALE * LOG2E)).astype(BF16)
            triples.append(jnp.concatenate([queries, triple[CH : 3 * CH].astype(BF16)], axis=0))
        for triple in triples:
            for h in range(HEADS):
                query = triple[h * WIDTH : (h + 1) * WIDTH]
                keys = triple[CH + h * WIDTH : CH + (h + 1) * WIDTH]
                at = pl.ds(pl.multiple_of((h * ZONES + zone) * PLACES, PLACES), PLACES)
                bias = jnp.concatenate([bias_ref[0, at, :], bias_ref[1, at, 0:16]], axis=1)
                scores.append(dot(keys, query, 0, 0) + bias)
        for score in scores:
            weights = jnp.exp2(score - jnp.max(score, axis=0, keepdims=True))
            softs.append((weights.astype(BF16), 1.0 / jnp.sum(weights, axis=0, keepdims=True)))
        for side, w in enumerate(windows):
            merged = []
            for h in range(HEADS):
                weights, inv = softs[side * HEADS + h]
                values = triples[side][2 * CH + h * WIDTH : 2 * CH + (h + 1) * WIDTH]
                merged.append((dot(values, weights) * inv).astype(BF16))
            merged = jnp.concatenate(merged, axis=0)
            mrg_s[w] = merged
            attended = dot(merged, wproj_ref[...], 0, 0).astype(BF16).astype(F32)
            resid_s[w] = (win[0, w] + attended).astype(BF16)
        for side, w in enumerate(windows):
            trip_s[w] = triples[side]
            for h in range(HEADS):
                weights, inv = softs[side * HEADS + h]
                soft_s[w * HEADS + h] = weights
                inv_s[w, h : h + 1] = inv
        return carry

    lax.fori_loop(0, ZONES, forward, 0)

    many = 4
    chunk = many * PLACES

    def feed_forward(c, carry):
        here = pl.ds(c * many, many)
        resid = resid_s[here].reshape(chunk, CH).astype(F32)
        up_f = win[1, here].reshape(chunk, CH)
        up = up_f.astype(BF16)
        unit, rscale = normed(resid)
        second = unit * g2
        pre = dot(second.astype(BF16), wup_ref[...])
        c0, c1 = 0.7978845608028654, 0.7978845608028654 * 0.044715
        sq = pre * pre
        tanh = jnp.tanh(pre * (c0 + c1 * sq))
        half = 0.5 + 0.5 * tanh
        hidden = (pre * half).astype(BF16)
        slope = half + half * (1.0 - tanh) * pre * (c0 + (3.0 * c1) * sq)
        upd_s[here] = (resid + dot(hidden, wdown_ref[...], 1, 1)).reshape(many, PLACES, CH)
        ddown_s[...] += dot(jnp.transpose(up_f).astype(BF16), hidden)
        d_pre = (slope * dot(up, wdown_ref[...])).astype(BF16)
        dup_s[...] += dot(jnp.transpose(second).astype(BF16), d_pre)
        d_norm = dot(d_pre, wup_ref[...], 1, 1)
        d_in = norm_back(unit, rscale, g2, d_norm)
        dres_s[here] = (d_in + up_f).reshape(many, PLACES, CH)
        return carry

    lax.fori_loop(0, WINDOWS // many, feed_forward, 0)

    for i in range(6):
        put(part, 12 * i, dup_s[:, 128 * i : 128 * i + 128] * grad_scale)
        put(part, 72 + 12 * i, ddown_s[:, 128 * i : 128 * i + 128] * grad_scale)
    early = AllReduce(EARLY, part, full, spot, early_bufs)
    late = AllReduce(LATE, part, full, spot, late_bufs)
    early.step(0)

    cut_back(upd_s, 0, grid, band, side, corner)
    back_pairs = ((band, band_s2, band_r2), (side, side_s2, side_r2), (corner, corner_s2, corner_r2))

    def back_copies(f):
        return [
            remote(
                src.at[f], dst.at[f], back_sems.at[0, f, i], back_sems.at[1, f, i], spot.after[i]
            )
            for i, (_, src, dst) in enumerate(back_pairs)
        ]

    for source, target, _ in back_pairs:
        target[0] = source[0].astype(BF16)
    start(back_copies(0))

    def backward_scores(zone, carry):
        windows = [zone * 2, zone * 2 + 1]
        leans, d_scores = [], []
        for w in windows:
            d_merged = dot(wproj_ref[...], dres_s[w].astype(BF16), 1, 1)
            for h in range(HEADS):
                at = slice(h * WIDTH, (h + 1) * WIDTH)
                d_m = d_merged[at] * inv_s[w, h : h + 1]
                lean = jnp.sum(d_m * mrg_s[w, at].astype(F32), axis=0, keepdims=True)
                leans.append((d_m.astype(BF16), lean))
        for side, w in enumerate(windows):
            for h in range(HEADS):
                d_m, lean = leans[side * HEADS + h]
                values = trip_s[w, 2 * CH + h * WIDTH : 2 * CH + (h + 1) * WIDTH]
                d_chances = dot(values, d_m, 0, 0)
                d_scores.append(soft_s[w * HEADS + h].astype(F32) * (d_chances - lean))
        for h in range(HEADS):
            at = pl.ds(pl.multiple_of((h * ZONES + zone) * PLACES, PLACES), PLACES)
            both = d_scores[h] + d_scores[HEADS + h]
            ds_ref[0, at, :] = both[:, 0:128]
            ds_ref[1, at, 0:16] = both[:, 128:PLACES]
        for side, w in enumerate(windows):
            for h in range(HEADS):
                dsoft_s[w * HEADS + h] = d_scores[side * HEADS + h].astype(BF16)
                dmrg_s[w, h * WIDTH : (h + 1) * WIDTH] = leans[side * HEADS + h][0]
        pl.when(zone == 1)(functools.partial(early.step, 1))
        return carry

    lax.fori_loop(0, ZONES, backward_scores, 0)

    def scatter_groups(turn, carry):
        step = functools.partial(scatter_step, ds_ref, idx_ref, hot_ref, acc_ref)
        lax.fori_loop(turn * 3, turn * 3 + 3, step, 0)
        pl.when(turn == 1)(functools.partial(early.step, 2))
        pl.when(turn == 4)(functools.partial(early.step, 3))
        return carry

    lax.fori_loop(0, 6, scatter_groups, 0)

    lon = spot.lon
    for i in range(PAIRS):
        tab_s[i] = (acc_ref[48 * i : 48 * i + 48] * grad_scale).astype(BF16)
    tab_s[PAIRS] = jnp.zeros((48, 256), BF16)

    def table_scatter():
        return [
            remote(
                tab_s.at[lax.rem(lon + d + 1, 8)],
                tab_r.at[d],
                tab_sems.at[0, d],
                tab_sems.at[1, d],
                spot.along_lon[d],
            )
            for d in range(7)
        ]

    def table_gather():
        return [
            remote(
                tab_full.at[lon],
                tab_full.at[lon],
                tab_sems.at[2, d],
                tab_sems.at[3, d],
                spot.along_lon[d],
            )
            for d in range(7)
        ]

    start(table_scatter())

    def backward_triple(zone, carry):
        windows = [zone * 2, zone * 2 + 1]
        for w in windows:
            out = []
            for h in range(HEADS):
                keys = trip_s[w, CH + h * WIDTH : CH + (h + 1) * WIDTH]
                out.append((dot(keys, dsoft_s[w * HEADS + h]) * SCALE).astype(BF16))
            for h in range(HEADS):
                query = trip_s[w, h * WIDTH : (h + 1) * WIDTH]
                d_keys = dot(query, dsoft_s[w * HEADS + h], 1, 1)
                out.append((d_keys * (1 / LOG2E)).astype(BF16))
            for h in range(HEADS):
                d_m = dmrg_s[w, h * WIDTH : (h + 1) * WIDTH]
                out.append(dot(d_m, soft_s[w * HEADS + h], 1, 1).astype(BF16))
            d_triple = jnp.concatenate(out, axis=0)
            first_t = jnp.transpose(first_s[w].astype(F32)).astype(BF16)
            dqkv_s[...] += dot(first_t, d_triple, 1, 1)
            dproj_s[...] += dot(mrg_s[w], dres_s[w].astype(BF16))
            dtrip_s[w] = d_triple
        pl.when(zone == 1)(functools.partial(early.step, 4))
        return carry

    lax.fori_loop(0, ZONES, backward_triple, 0)

    for i in range(4):
        put(part, 144 + 12 * i, dqkv_s[:, 128 * i : 128 * i + 128] * grad_scale)
    mixed = jnp.concatenate([dqkv_s[:, 512:576], dproj_s[:, 0:64]], axis=1)
    put(part, 192, mixed * grad_scale)
    put(part, 204, dproj_s[:, 64:192] * grad_scale)
    part[216:TILES] = jnp.zeros((TILES - 216, 16, 128), BF16)
    late.step(0)
    finish(table_scatter())
    total = tab_s[lon].astype(F32)
    for d in range(7):
        total += tab_r[d].astype(F32)
    tab_full[lon] = total.astype(BF16)
    start(table_gather())

    def backward_norm(zone, carry):
        for w in (zone * 2, zone * 2 + 1):
            d_first = dot(dtrip_s[w], wqkvt_s[...], 0, 0).astype(BF16).astype(F32)
            unit, rscale = normed(win[0, w])
            d_in = norm_back(unit, rscale, g1, d_first)
            upd_s[w] = dres_s[w] + d_in
        return carry

    lax.fori_loop(0, 2, backward_norm, 0)
    late.step(1)
    lax.fori_loop(2, ZONES, backward_norm, 0)
    cut_back(upd_s, 1, grid, band, side, corner)
    for source, target, _ in back_pairs:
        target[1] = source[1].astype(BF16)
    start(back_copies(1))
    early.step(5)
    finish(back_copies(0))
    add_back(0, grid, band_r2, side_r2, corner_r2)
    for i in range(6):
        updo_ref[:, i] = (grid[0, :, i] * valid[i]).astype(BF16)
    late.step(2)
    finish(back_copies(1))
    add_back(1, grid, band_r2, side_r2, corner_r2)
    late.step(3)
    for i in range(6):
        dtoko_ref[:, i] = (grid[1, :, i] * valid[i]).astype(BF16)
    full_ref[0:128] = full[0:128]
    finish(table_gather())
    tab_ref[...] = tab_full[...]
    late.step(4)
    late.step(5)
    full_ref[128:TILES] = full[128:TILES]


def block_pass(grad_scale, *args):
    sd = jax.ShapeDtypeStruct
    sem = pltpu.SemaphoreType.DMA
    return pl.pallas_call(
        functools.partial(block_kernel, grad_scale),
        out_shape=[
            sd((8, 6, 24, CH), BF16),
            sd((8, 6, 24, CH), BF16),
            sd((TILES, 16, 128), BF16),
            sd((8, 48, 256), BF16),
        ],
        in_specs=[pl.BlockSpec(memory_space=pltpu.SMEM)] + [VMEM_SPEC] * 10,
        out_specs=[VMEM_SPEC] * 4,
        scratch_shapes=[
            vm((PLACES, 256), jnp.int32),
            vm((HI * ROWS, 256), F32),
            vm((GROUPS, 256, SPAN), BF16),
            vm((2, ROWS * PLACES, 128), F32),
            vm((PAIRS * 48, 256), F32),
            vm((2, WINDOWS, PLACES, CH), F32),
            vm((2, 8, 6, 24, CH), F32),
            *piece_scratch(),
            vm((3 * CH, CH), BF16),
            vm((WINDOWS * HEADS, PLACES, PLACES), BF16),
            vm((WINDOWS, 3 * CH, PLACES), BF16),
            vm((WINDOWS, CH, PLACES), BF16),
            vm((WINDOWS, 8, PLACES), F32),
            vm((WINDOWS, PLACES, CH), BF16),
            vm((WINDOWS, PLACES, CH), BF16),
            vm((WINDOWS, PLACES, CH), F32),
            vm((WINDOWS, 3 * CH, PLACES), BF16),
            vm((WINDOWS * HEADS, PLACES, PLACES), BF16),
            vm((WINDOWS, CH, PLACES), BF16),
            vm((WINDOWS, PLACES, CH), F32),
            vm((CH, 3 * CH), F32),
            vm((CH, CH), F32),
            vm((CH, HIDDEN), F32),
            vm((CH, HIDDEN), F32),
            vm((TILES, 16, 128), BF16),
            vm((TILES, 16, 128), BF16),
            all_reduce_scratch(EARLY),
            all_reduce_scratch(LATE),
            vm((8, 48, 256), BF16),
            vm((7, 48, 256), BF16),
            vm((8, 48, 256), BF16),
            sem((2, 3)),
            sem((2, 2, 3)),
            sem((4, 7)),
        ],
        compiler_params=pltpu.CompilerParams(
            vmem_limit_bytes=LIMIT, collective_id=0, has_side_effects=True
        ),
    )(*args)


def write_kernel(
    upd_ref, dtok_ref, full_ref, tab_ref, g1_ref, wqkv_ref, g2_ref, wup_ref,
    updo_ref, dtoko_ref, gain1_ref, qkv_ref, proj_ref, gain2_ref, up_ref, down_ref, table_ref,
):
    updo_ref[...] = upd_ref[...]
    dtoko_ref[...] = dtok_ref[...]

    def get(tile):
        return full_ref[tile : tile + 12].reshape(192, 128).astype(F32)

    for i in range(6):
        up_ref[:, 128 * i : 128 * i + 128] = get(12 * i)
        down_ref[:, 128 * i : 128 * i + 128] = get(72 + 12 * i)
    for i in range(4):
        qkv_ref[:, 128 * i : 128 * i + 128] = get(144 + 12 * i)
    mixed = get(192)
    qkv_ref[:, 512:576] = mixed[:, 0:64]
    proj_ref[...] = jnp.concatenate([mixed[:, 64:128], get(204)], axis=1)
    for weight, d_weight, gain, out in (
        (wqkv_ref, qkv_ref, g1_ref, gain1_ref),
        (wup_ref, up_ref, g2_ref, gain2_ref),
    ):
        sums = jnp.sum(weight[...].astype(F32) * d_weight[...], axis=1, keepdims=True)
        row = jnp.transpose(jnp.broadcast_to(sums, (CH, 128)))[0]
        out[...] = row / gain[...].astype(F32)
    for hi in range(HI):
        wide = min(256, ENTRIES - hi * 256)
        block = tab_ref[hi // 2].astype(F32)[hi % 2 * ROWS : (hi % 2 + 1) * ROWS]
        for head in range(HEADS):
            table_ref[head, :, hi * 256 : hi * 256 + wide] = block[
                head * ZONES : (head + 1) * ZONES, 0:wide
            ]


def write_out(*args):
    sd = jax.ShapeDtypeStruct
    return pl.pallas_call(
        write_kernel,
        out_shape=[
            sd((8, 6, 24, CH), BF16),
            sd((8, 6, 24, CH), BF16),
            sd((CH,), F32),
            sd((CH, 3 * CH), F32),
            sd((CH, CH), F32),
            sd((CH,), F32),
            sd((CH, HIDDEN), F32),
            sd((CH, HIDDEN), F32),
            sd((HEADS, ZONES, ENTRIES), F32),
        ],
        in_specs=[VMEM_SPEC] * 8,
        out_specs=[VMEM_SPEC] * 9,
        compiler_params=pltpu.CompilerParams(vmem_limit_bytes=LIMIT),
    )(*args)


def per_device(
    tokens,
    lat_valid,
    gain_attn,
    w_qkv,
    w_proj,
    gain_mlp,
    w_up,
    w_down,
    bias_table,
    index_table,
    cotangent,
):
    levels, row_count, col_count, channels = tokens.shape
    grad_scale = float(levels * row_count * col_count * 128) ** (-0.5)
    parts = block_pass(
        grad_scale,
        lat_valid,
        tokens,
        cotangent,
        bias_table.transpose(1, 0, 2),
        index_table,
        gain_attn,
        w_qkv,
        w_proj,
        gain_mlp,
        w_up,
        w_down.T,
    )
    updated, d_tokens, d_gain1, d_qkv, d_proj, d_gain2, d_up, d_down, d_table = write_out(
        *parts, gain_attn, w_qkv, gain_mlp, w_up
    )
    d_table = d_table.transpose(1, 0, 2)
    return updated, d_tokens, d_gain1, d_qkv, d_proj, d_gain2, d_up, d_down.T, d_table


def solution(mesh):
    field = P(None, "lat", "lon", None)
    in_specs = (field, P("lat"), P(), P(), P(), P(), P(), P(), P("lat"), P(), field)
    out_specs = (field, field, P(), P(), P(), P(), P(), P(), P("lat"))
    return jax.shard_map(
        per_device, mesh=mesh, in_specs=in_specs, out_specs=out_specs, check_vma=False
    )
```

time: 104 us -> 81.1 us (0.78); the launches traced: 104 us -> 79.6 us
  Pallas kernels: 103 us -> 79 us
    pallas_call x1, Pallas kernels: 99.6 us -> 75.4 us  [block_pass(): pl.pallas_call(functools.partial(block_kernel, grad_scale), out_shape=[sd...]
where the time goes in v4:
time: 81.1 us; the launch traced here: 79.6 us
  Pallas kernels  79 us (97%)
    pallas_call x1, Pallas kernels, block_pass(): pl.pallas_call(functools.partial(block_kernel, grad_scale), out_shape=[sd...  75.4 us
    pallas_call x1, Pallas kernels, write_out(): pl.pallas_call(write_kernel, out_shape=[sd((8, 6, 24, CH), BF16), sd((8,...  3.58 us

profile of v4, /device:TPU:0, one launch (start us, length us, event | category | flops | bytes accessed | tf_op | source)
XLA Modules:
  0.0 79.6 jit_solution(3520515631769948606)
XLA Ops:
  0.6 75.4 %shard_map.178 = (bf16[8,6,24,192]{3,2,1,0:T(8,128)(2,1)}, bf16[8,6,24,192]{3,2,1,0:T(8,128)(2,1)}, bf16[224,16,128]{2,1,0:T(8,128)(2,1)}, bf16[8,48,256]{2,1,0:T(8,128)(2,1)}) custom-call(s32[6]{0:T(128)} %valid_ref.1, bf16[8,6,24,192]{3,2,1,0:T(8,128)(2,1)} %tok_ref.1, bf16[8,6,24,192]{3,2,1,0:T(8,128)(2,1)} %cot_ref.1, f32[6,4,3312]{2,1,0:T(4,128)} %bitcast.4, ...), custom_call_target="tpu_custom_call" | custom-call | tf_op jit(solution)/shard_map/pallas_call | solution.py:668
  76.0 3.6 %shard_map.179 = (bf16[8,6,24,192]{3,2,1,0:T(8,128)(2,1)}, bf16[8,6,24,192]{3,2,1,0:T(8,128)(2,1)}, f32[192]{0:T(256)}, f32[192,576]{1,0:T(8,128)}, f32[192,192]...) custom-call(bf16[8,6,24,192]{3,2,1,0:T(8,128)(2,1)} %get-tuple-element.22.upd_ref, ...), custom_call_target="tpu_custom_call" | custom-call | tf_op jit(solution)/shard_map/pallas_call | solution.py:756

commit v5 on v4

--- a/solution.py
+++ b/solution.py
@@ -106,7 +106,7 @@
             bias_ref[1, pl.ds(key, ROWS, stride=PLACES), :] = rest_i
         return carry
 
-    lax.fori_loop(0, GROUPS, step, 0)
+    return step
 
 
 def scatter_step(ds_ref, idx_ref, hot_ref, acc_ref, group, carry):
@@ -415,6 +415,8 @@
     cut_pieces(cot_ref, 1, valid, win, band, side, corner)
     for source, target in ((band, band_s), (side, side_s), (corner, corner_s)):
         target[...] = source[...].astype(BF16)
+    gather = gather_bias(table_ref, idx_in, bias_ref, idx_ref, t2_ref, hot_ref)
+    lax.fori_loop(0, 10, gather, 0)
     pl.semaphore_wait(barrier, len(spot.all))
     pairs = ((band_s, band_r), (side_s, side_r), (corner_s, corner_r))
     halo = [
@@ -422,7 +424,7 @@
         for i, (src, dst) in enumerate(pairs)
     ]
     start(halo)
-    gather_bias(table_ref, idx_in, bias_ref, idx_ref, t2_ref, hot_ref)
+    lax.fori_loop(10, GROUPS, gather, 0)
     wqkvt_s[...] = jnp.transpose(wqkv_ref[...].astype(F32)).astype(BF16)
     g1 = g1_ref[...].astype(F32).reshape(1, CH)
     g2 = g2_ref[...].astype(F32).reshape(1, CH)
@@ -550,46 +552,6 @@
 
     lax.fori_loop(0, ZONES, backward_scores, 0)
 
-    def scatter_groups(turn, carry):
-        step = functools.partial(scatter_step, ds_ref, idx_ref, hot_ref, acc_ref)
-        lax.fori_loop(turn * 3, turn * 3 + 3, step, 0)
-        pl.when(turn == 1)(functools.partial(early.step, 2))
-        pl.when(turn == 4)(functools.partial(early.step, 3))
-        return carry
-
-    lax.fori_loop(0, 6, scatter_groups, 0)
-
-    lon = spot.lon
-    for i in range(PAIRS):
-        tab_s[i] = (acc_ref[48 * i : 48 * i + 48] * grad_scale).astype(BF16)
-    tab_s[PAIRS] = jnp.zeros((48, 256), BF16)
-
-    def table_scatter():
-        return [
-            remote(
-                tab_s.at[lax.rem(lon + d + 1, 8)],
-                tab_r.at[d],
-                tab_sems.at[0, d],
-                tab_sems.at[1, d],
-                spot.along_lon[d],
-            )
-            for d in range(7)
-        ]
-
-    def table_gather():
-        return [
-            remote(
-                tab_full.at[lon],
-                tab_full.at[lon],
-                tab_sems.at[2, d],
-                tab_sems.at[3, d],
-                spot.along_lon[d],
-            )
-            for d in range(7)
-        ]
-
-    start(table_scatter())
-
     def backward_triple(zone, carry):
         windows = [zone * 2, zone * 2 + 1]
         for w in windows:
@@ -609,7 +571,7 @@
             dqkv_s[...] += dot(first_t, d_triple, 1, 1)
             dproj_s[...] += dot(mrg_s[w], dres_s[w].astype(BF16))
             dtrip_s[w] = d_triple
-        pl.when(zone == 1)(functools.partial(early.step, 4))
+        pl.when(zone == 2)(functools.partial(early.step, 2))
         return carry
 
     lax.fori_loop(0, ZONES, backward_triple, 0)
@@ -621,12 +583,47 @@
     put(part, 204, dproj_s[:, 64:192] * grad_scale)
     part[216:TILES] = jnp.zeros((TILES - 216, 16, 128), BF16)
     late.step(0)
-    finish(table_scatter())
-    total = tab_s[lon].astype(F32)
-    for d in range(7):
-        total += tab_r[d].astype(F32)
-    tab_full[lon] = total.astype(BF16)
-    start(table_gather())
+    def scatter_groups(turn, carry):
+        step = functools.partial(scatter_step, ds_ref, idx_ref, hot_ref, acc_ref)
+        lax.fori_loop(turn * 3, turn * 3 + 3, step, 0)
+        pl.when(turn == 0)(functools.partial(late.step, 1))
+        pl.when(turn == 2)(functools.partial(early.step, 3))
+        pl.when(turn == 5)(functools.partial(late.step, 2))
+        return carry
+
+    lax.fori_loop(0, 6, scatter_groups, 0)
+
+    lon = spot.lon
+    for i in range(PAIRS):
+        tab_s[i] = (acc_ref[48 * i : 48 * i + 48] * grad_scale).astype(BF16)
+    tab_s[PAIRS] = jnp.zeros((48, 256), BF16)
+
+    def table_scatter():
+        return [
+            remote(
+                tab_s.at[lax.rem(lon + d + 1, 8)],
+                tab_r.at[d],
+                tab_sems.at[0, d],
+                tab_sems.at[1, d],
+                spot.along_lon[d],
+            )
+            for d in range(7)
+        ]
+
+    def table_gather():
+        return [
+            remote(
+                tab_full.at[lon],
+                tab_full.at[lon],
+                tab_sems.at[2, d],
+                tab_sems.at[3, d],
+                spot.along_lon[d],
+            )
+            for d in range(7)
+        ]
+
+    start(table_scatter())
+    early.step(4)
 
     def backward_norm(zone, carry):
         for w in (zone * 2, zone * 2 + 1):
@@ -636,28 +633,31 @@
             upd_s[w] = dres_s[w] + d_in
         return carry
 
-    lax.fori_loop(0, 2, backward_norm, 0)
-    late.step(1)
-    lax.fori_loop(2, ZONES, backward_norm, 0)
+    lax.fori_loop(0, ZONES, backward_norm, 0)
     cut_back(upd_s, 1, grid, band, side, corner)
     for source, target, _ in back_pairs:
         target[1] = source[1].astype(BF16)
     start(back_copies(1))
-    early.step(5)
+    late.step(3)
+    finish(table_scatter())
+    total = tab_s[lon].astype(F32)
+    for d in range(7):
+        total += tab_r[d].astype(F32)
+    tab_full[lon] = total.astype(BF16)
+    start(table_gather())
     finish(back_copies(0))
     add_back(0, grid, band_r2, side_r2, corner_r2)
     for i in range(6):
         updo_ref[:, i] = (grid[0, :, i] * valid[i]).astype(BF16)
-    late.step(2)
+    early.step(5)
+    full_ref[0:128] = full[0:128]
     finish(back_copies(1))
     add_back(1, grid, band_r2, side_r2, corner_r2)
-    late.step(3)
     for i in range(6):
         dtoko_ref[:, i] = (grid[1, :, i] * valid[i]).astype(BF16)
-    full_ref[0:128] = full[0:128]
+    late.step(4)
     finish(table_gather())
     tab_ref[...] = tab_full[...]
-    late.step(4)
     late.step(5)
     full_ref[128:TILES] = full[128:TILES]
 

time: 81.1 us -> 74.8 us (0.922)
  Pallas kernels: 79 us -> 72.9 us
    pallas_call x1, Pallas kernels: 75.4 us -> 69.4 us  [block_pass(): pl.pallas_call(functools.partial(block_kernel, grad_scale), out_shape=[sd...]
where the time goes in v5:
time: 74.8 us; the launch traced here: 73.6 us
  Pallas kernels  72.9 us (97%)
    pallas_call x1, Pallas kernels, block_pass(): pl.pallas_call(functools.partial(block_kernel, grad_scale), out_shape=[sd...  69.4 us
    pallas_call x1, Pallas kernels, write_out(): pl.pallas_call(write_kernel, out_shape=[sd((8, 6, 24, CH), BF16), sd((8,...  3.58 us

profile of v5, /device:TPU:0, one launch (start us, length us, event | category | flops | bytes accessed | tf_op | source)
XLA Modules:
  0.0 73.6 jit_solution(5163478194825865532)
XLA Ops:
  0.6 69.4 %shard_map.178 = (bf16[8,6,24,192]{3,2,1,0:T(8,128)(2,1)}, bf16[8,6,24,192]{3,2,1,0:T(8,128)(2,1)}, bf16[224,16,128]{2,1,0:T(8,128)(2,1)}, bf16[8,48,256]{2,1,0:T(8,128)(2,1)}) custom-call(s32[6]{0:T(128)} %valid_ref.1, bf16[8,6,24,192]{3,2,1,0:T(8,128)(2,1)} %tok_ref.1, bf16[8,6,24,192]{3,2,1,0:T(8,128)(2,1)} %cot_ref.1, f32[6,4,3312]{2,1,0:T(4,128)} %bitcast.4, ...), custom_call_target="tpu_custom_call" | custom-call | tf_op jit(solution)/shard_map/pallas_call | solution.py:668
  70.0 3.6 %shard_map.179 = (bf16[8,6,24,192]{3,2,1,0:T(8,128)(2,1)}, bf16[8,6,24,192]{3,2,1,0:T(8,128)(2,1)}, f32[192]{0:T(256)}, f32[192,576]{1,0:T(8,128)}, f32[192,192]...) custom-call(bf16[8,6,24,192]{3,2,1,0:T(8,128)(2,1)} %get-tuple-element.22.upd_ref, ...), custom_call_target="tpu_custom_call" | custom-call | tf_op jit(solution)/shard_map/pallas_call | solution.py:756

commit v6 on v5

--- a/solution.py
+++ b/solution.py
@@ -416,7 +416,7 @@
     for source, target in ((band, band_s), (side, side_s), (corner, corner_s)):
         target[...] = source[...].astype(BF16)
     gather = gather_bias(table_ref, idx_in, bias_ref, idx_ref, t2_ref, hot_ref)
-    lax.fori_loop(0, 10, gather, 0)
+    lax.fori_loop(0, 10, gather, 0, unroll=2)
     pl.semaphore_wait(barrier, len(spot.all))
     pairs = ((band_s, band_r), (side_s, side_r), (corner_s, corner_r))
     halo = [
@@ -424,7 +424,7 @@
         for i, (src, dst) in enumerate(pairs)
     ]
     start(halo)
-    lax.fori_loop(10, GROUPS, gather, 0)
+    lax.fori_loop(10, GROUPS, gather, 0, unroll=2)
     wqkvt_s[...] = jnp.transpose(wqkv_ref[...].astype(F32)).astype(BF16)
     g1 = g1_ref[...].astype(F32).reshape(1, CH)
     g2 = g2_ref[...].astype(F32).reshape(1, CH)
@@ -470,9 +470,8 @@
                 inv_s[w, h : h + 1] = inv
         return carry
 
-    lax.fori_loop(0, ZONES, forward, 0)
-
-    many = 4
+
+    many = 2
     chunk = many * PLACES
 
     def feed_forward(c, carry):
@@ -498,7 +497,13 @@
         dres_s[here] = (d_in + up_f).reshape(many, PLACES, CH)
         return carry
 
-    lax.fori_loop(0, WINDOWS // many, feed_forward, 0)
+    def feed_and_forward(zone, carry):
+        feed_forward(zone - 1, carry)
+        return forward(zone, carry)
+
+    forward(0, 0)
+    lax.fori_loop(1, ZONES, feed_and_forward, 0)
+    feed_forward(ZONES - 1, 0)
 
     for i in range(6):
         put(part, 12 * i, dup_s[:, 128 * i : 128 * i + 128] * grad_scale)
@@ -585,7 +590,8 @@
     late.step(0)
     def scatter_groups(turn, carry):
         step = functools.partial(scatter_step, ds_ref, idx_ref, hot_ref, acc_ref)
-        lax.fori_loop(turn * 3, turn * 3 + 3, step, 0)
+        for i in range(3):
+            step(turn * 3 + i, 0)
         pl.when(turn == 0)(functools.partial(late.step, 1))
         pl.when(turn == 2)(functools.partial(early.step, 3))
         pl.when(turn == 5)(functools.partial(late.step, 2))

time: 74.8 us -> 72 us (0.963)
  Pallas kernels: 72.9 us -> 70.6 us
    pallas_call x1, Pallas kernels: 69.4 us -> 67 us  [block_pass(): pl.pallas_call(functools.partial(block_kernel, grad_scale), out_shape=[sd...]
where the time goes in v6:
time: 72 us; the launch traced here: 71.3 us
  Pallas kernels  70.6 us (98%)
    pallas_call x1, Pallas kernels, block_pass(): pl.pallas_call(functools.partial(block_kernel, grad_scale), out_shape=[sd...  67 us
    pallas_call x1, Pallas kernels, write_out(): pl.pallas_call(write_kernel, out_shape=[sd((8, 6, 24, CH), BF16), sd((8,...  3.58 us

profile of v6, /device:TPU:0, one launch (start us, length us, event | category | flops | bytes accessed | tf_op | source)
XLA Modules:
  0.0 71.3 jit_solution(12115248006586558171)
XLA Ops:
  0.6 67.0 %shard_map.178 = (bf16[8,6,24,192]{3,2,1,0:T(8,128)(2,1)}, bf16[8,6,24,192]{3,2,1,0:T(8,128)(2,1)}, bf16[224,16,128]{2,1,0:T(8,128)(2,1)}, bf16[8,48,256]{2,1,0:T(8,128)(2,1)}) custom-call(s32[6]{0:T(128)} %valid_ref.1, bf16[8,6,24,192]{3,2,1,0:T(8,128)(2,1)} %tok_ref.1, bf16[8,6,24,192]{3,2,1,0:T(8,128)(2,1)} %cot_ref.1, f32[6,4,3312]{2,1,0:T(4,128)} %bitcast.4, ...), custom_call_target="tpu_custom_call" | custom-call | tf_op jit(solution)/shard_map/pallas_call | solution.py:674
  67.7 3.6 %shard_map.179 = (bf16[8,6,24,192]{3,2,1,0:T(8,128)(2,1)}, bf16[8,6,24,192]{3,2,1,0:T(8,128)(2,1)}, f32[192]{0:T(256)}, f32[192,576]{1,0:T(8,128)}, f32[192,192]...) custom-call(bf16[8,6,24,192]{3,2,1,0:T(8,128)(2,1)} %get-tuple-element.22.upd_ref, ...), custom_call_target="tpu_custom_call" | custom-call | tf_op jit(solution)/shard_map/pallas_call | solution.py:762

commit v7 on v6

--- a/solution.py
+++ b/solution.py
@@ -195,22 +195,21 @@
                     win[f, 2 * zone + 1, at : at + 6] = row[18:24]
 
 
-def add_pieces(win, band, side, corner):
-    for f in range(2):
-        band_v = band[f].astype(F32)
-        side_v = side[f].astype(F32)
-        corner_v = corner[f].astype(F32)
-        for zone in range(ZONES):
-            for depth in range(2):
-                for i in range(3):
-                    piece = depth * 3 + i
-                    at = (depth * 6 + i) * 12
-                    win[f, 2 * zone + 1, at + 6 : at + 12] = side_v[spot_of(zone, piece, 6)]
-                    at = (depth * 6 + i + 3) * 12
-                    rows = band_v[spot_of(zone, piece, 18)]
-                    win[f, 2 * zone, at : at + 12] = rows[0:12]
-                    win[f, 2 * zone + 1, at : at + 6] = rows[12:18]
-                    win[f, 2 * zone + 1, at + 6 : at + 12] = corner_v[spot_of(zone, piece, 6)]
+def add_pieces(f, win, band, side, corner):
+    band_v = band[f].astype(F32)
+    side_v = side[f].astype(F32)
+    corner_v = corner[f].astype(F32)
+    for zone in range(ZONES):
+        for depth in range(2):
+            for i in range(3):
+                piece = depth * 3 + i
+                at = (depth * 6 + i) * 12
+                win[f, 2 * zone + 1, at + 6 : at + 12] = side_v[spot_of(zone, piece, 6)]
+                at = (depth * 6 + i + 3) * 12
+                rows = band_v[spot_of(zone, piece, 18)]
+                win[f, 2 * zone, at : at + 12] = rows[0:12]
+                win[f, 2 * zone + 1, at : at + 6] = rows[12:18]
+                win[f, 2 * zone + 1, at + 6 : at + 12] = corner_v[spot_of(zone, piece, 6)]
 
 
 def cut_back(field, f, grid, band, side, corner):
@@ -420,18 +419,25 @@
     pl.semaphore_wait(barrier, len(spot.all))
     pairs = ((band_s, band_r), (side_s, side_r), (corner_s, corner_r))
     halo = [
-        remote(src, dst, halo_sems.at[0, i], halo_sems.at[1, i], spot.before[i])
-        for i, (src, dst) in enumerate(pairs)
+        [
+            remote(
+                src.at[f], dst.at[f], halo_sems.at[0, f, i], halo_sems.at[1, f, i], spot.before[i]
+            )
+            for i, (src, dst) in enumerate(pairs)
+        ]
+        for f in range(2)
     ]
-    start(halo)
-    lax.fori_loop(10, GROUPS, gather, 0, unroll=2)
+    start(halo[0])
+    lax.fori_loop(10, 14, gather, 0, unroll=2)
+    start(halo[1])
+    lax.fori_loop(14, GROUPS, gather, 0, unroll=2)
     wqkvt_s[...] = jnp.transpose(wqkv_ref[...].astype(F32)).astype(BF16)
     g1 = g1_ref[...].astype(F32).reshape(1, CH)
     g2 = g2_ref[...].astype(F32).reshape(1, CH)
     for ref in (dqkv_s, dproj_s, dup_s, ddown_s, acc_ref):
         ref[...] = jnp.zeros_like(ref)
-    finish(halo)
-    add_pieces(win, band_r, side_r, corner_r)
+    finish(halo[0])
+    add_pieces(0, win, band_r, side_r, corner_r)
 
     def forward(zone, carry):
         windows = [zone * 2, zone * 2 + 1]
@@ -502,6 +508,8 @@
         return forward(zone, carry)
 
     forward(0, 0)
+    finish(halo[1])
+    add_pieces(1, win, band_r, side_r, corner_r)
     lax.fori_loop(1, ZONES, feed_and_forward, 0)
     feed_forward(ZONES - 1, 0)
 
@@ -637,6 +645,7 @@
             unit, rscale = normed(win[0, w])
             d_in = norm_back(unit, rscale, g1, d_first)
             upd_s[w] = dres_s[w] + d_in
+        pl.when(zone == 2)(functools.partial(late.step, 3))
         return carry
 
     lax.fori_loop(0, ZONES, backward_norm, 0)
@@ -644,7 +653,6 @@
     for source, target, _ in back_pairs:
         target[1] = source[1].astype(BF16)
     start(back_copies(1))
-    late.step(3)
     finish(table_scatter())
     total = tab_s[lon].astype(F32)
     for d in range(7):
@@ -713,7 +721,7 @@
             vm((8, 48, 256), BF16),
             vm((7, 48, 256), BF16),
             vm((8, 48, 256), BF16),
-            sem((2, 3)),
+            sem((2, 2, 3)),
             sem((2, 2, 3)),
             sem((4, 7)),
         ],

time: 72 us -> 70.6 us (0.981)
  Pallas kernels: 70.6 us -> 68.8 us
    pallas_call x1, Pallas kernels: 67 us -> 65.2 us  [block_pass(): pl.pallas_call(functools.partial(block_kernel, grad_scale), out_shape=[sd...]
where the time goes in v7:
time: 70.6 us; the launch traced here: 69.4 us
  Pallas kernels  68.8 us (97%)
    pallas_call x1, Pallas kernels, block_pass(): pl.pallas_call(functools.partial(block_kernel, grad_scale), out_shape=[sd...  65.2 us
    pallas_call x1, Pallas kernels, write_out(): pl.pallas_call(write_kernel, out_shape=[sd((8, 6, 24, CH), BF16), sd((8,...  3.58 us

profile of v7, /device:TPU:0, one launch (start us, length us, event | category | flops | bytes accessed | tf_op | source)
XLA Modules:
  0.0 69.4 jit_solution(14746998572605272873)
XLA Ops:
  0.6 65.2 %shard_map.178 = (bf16[8,6,24,192]{3,2,1,0:T(8,128)(2,1)}, bf16[8,6,24,192]{3,2,1,0:T(8,128)(2,1)}, bf16[224,16,128]{2,1,0:T(8,128)(2,1)}, bf16[8,48,256]{2,1,0:T(8,128)(2,1)}) custom-call(s32[6]{0:T(128)} %valid_ref.1, bf16[8,6,24,192]{3,2,1,0:T(8,128)(2,1)} %tok_ref.1, bf16[8,6,24,192]{3,2,1,0:T(8,128)(2,1)} %cot_ref.1, f32[6,4,3312]{2,1,0:T(4,128)} %bitcast.4, ...), custom_call_target="tpu_custom_call" | custom-call | tf_op jit(solution)/shard_map/pallas_call | solution.py:682
  65.8 3.6 %shard_map.179 = (bf16[8,6,24,192]{3,2,1,0:T(8,128)(2,1)}, bf16[8,6,24,192]{3,2,1,0:T(8,128)(2,1)}, f32[192]{0:T(256)}, f32[192,576]{1,0:T(8,128)}, f32[192,192]...) custom-call(bf16[8,6,24,192]{3,2,1,0:T(8,128)(2,1)} %get-tuple-element.22.upd_ref, ...), custom_call_target="tpu_custom_call" | custom-call | tf_op jit(solution)/shard_map/pallas_call | solution.py:770
